TPU v7x, 32 devices: a whole 2x2x4 slice. The times are simulated.
32 devices in a mesh: lon: 4 (over z), lat: 2 (over x), dp: 4 (over y, core).
Axes of the slice: x: 2, y: 2, z: 4, core: 2. Of those that a mesh axis runs over, the one named last changes fastest.
Arguments:
- fields: bfloat16 [4, 256, 16, 512], P('dp', None, 'lat', 'lon'), may hold values from -6 to 6
- weight_one: bfloat16 [9, 256, 256], replicated, may hold values from -0.125 to 0.125
- weight_two: bfloat16 [9, 256, 256], replicated, may hold values from -0.125 to 0.125
- edge_flips: int32 [1, 4], replicated, may hold values from 0 to 1, as said below
- cotangent: bfloat16 [4, 256, 16, 512], P('dp', None, 'lat', 'lon'), may hold values from -6 to 6
Outputs:
- output: bfloat16 [4, 256, 16, 512], P('dp', None, 'lat', 'lon')
- grad_fields: bfloat16 [4, 256, 16, 512], P('dp', None, 'lat', 'lon')
- grad_one: float32 [9, 256, 256], replicated
- grad_two: float32 [9, 256, 256], replicated
Inputs may be any that keep to these rules, and one draw needn't show every extreme that they name: `edge_flips`: 0 on every edge inside a face; only row 2 // 2 - 1, the boundary between the band's two face rows, may hold 1, where the two faces meeting at that longitude tile store longitude in opposite orders.
All inputs are finite; a program needn't handle non-finite values.
Results may differ from a plain program's by a relative error of at most 0.0034.
Values may be sent and summed in bfloat16 or wider, within the bound.
A program may use at most 128 MiB of HBM per device.

v0:
```python
import jax
import jax.numpy as jnp
from jax import lax
from jax.sharding import PartitionSpec as P


def with_halo(cells, sides, width, closed):
    for axis, dim in sides:
        count = lax.axis_size(axis)
        ends = count if closed else count - 1
        head = lax.slice_in_dim(cells, 0, width, axis=dim)
        tail = lax.slice_in_dim(cells, cells.shape[dim] - width, cells.shape[dim], axis=dim)
        cells = jnp.concatenate(
            [
                lax.ppermute(tail, axis, [(i, (i + 1) % count) for i in range(ends)]),
                cells,
                lax.ppermute(head, axis, [((i + 1) % count, i) for i in range(ends)]),
            ],
            axis=dim,
        )
    return cells


def oriented(line_cells, reverse_flag):
    return jnp.where(reverse_flag == 1, jnp.flip(line_cells, -1), line_cells)


def edge_flags(edge_flips):
    lat_index = lax.axis_index("lat")
    lon_index = lax.axis_index("lon")
    lat_count = lax.axis_size("lat")
    upper_flip = lax.dynamic_slice(edge_flips, (jnp.maximum(lat_index - 1, 0), lon_index), (1, 1))[
        0, 0
    ]
    lower_flip = lax.dynamic_slice(
        edge_flips, (jnp.minimum(lat_index, lat_count - 2), lon_index), (1, 1)
    )[0, 0]
    return (upper_flip, lower_flip, lat_index > 0, lat_index < lat_count - 1)


def padded(source, edge_info):
    upper_flip, lower_flip, has_upper, has_lower = edge_info
    extended = with_halo(source, (("lon", 3), ("lat", 2)), 1, True)
    top_rim = jnp.where(has_upper, extended[:, :, 0, :], jnp.zeros_like(extended[:, :, 0, :]))
    bottom = jnp.where(has_lower, extended[:, :, -1, :], jnp.zeros_like(extended[:, :, -1, :]))
    top_rim = oriented(top_rim, upper_flip)
    bottom = oriented(bottom, lower_flip)
    return jnp.concatenate(
        [top_rim[:, :, None, :], extended[:, :, 1:-1, :], bottom[:, :, None, :]], 2
    )


def patches_of(padded_in, tile_rows, tile_cols):
    return jnp.stack(
        [
            padded_in[:, :, tap_row : tap_row + tile_rows, tap_col : tap_col + tile_cols]
            for tap_row in range(3)
            for tap_col in range(3)
        ],
        1,
    )


def convolve(patches, weight):
    return jnp.einsum("toc,btchw->bohw", weight, patches, preferred_element_type=jnp.float32)


def transposed(grad_tile, weight, tile_rows, tile_cols):
    batch, chans = (grad_tile.shape[0], weight.shape[2])
    padded_grad = jnp.zeros((batch, chans, tile_rows + 2, tile_cols + 2), jnp.float32)
    for tap_row in range(3):
        for tap_col in range(3):
            tap_term = jnp.einsum(
                "oc,bohw->bchw",
                weight[3 * tap_row + tap_col],
                grad_tile,
                preferred_element_type=jnp.float32,
            )
            padded_grad = padded_grad.at[
                :, :, tap_row : tap_row + tile_rows, tap_col : tap_col + tile_cols
            ].add(tap_term)
    return padded_grad


def returned(padded_grad, edge_info):
    upper_flip, lower_flip, has_upper, has_lower = edge_info
    top_rim = oriented(padded_grad[:, :, 0, :], upper_flip)
    bottom = oriented(padded_grad[:, :, -1, :], lower_flip)
    rim_rows = jnp.stack([top_rim, bottom], 2)
    received = with_halo(rim_rows, (("lat", 2),), 1, False)
    interior = padded_grad[:, :, 1:-1, :]
    interior = interior.at[:, :, 0, :].add(received[:, :, 0, :])
    interior = interior.at[:, :, -1, :].add(received[:, :, -1, :])
    side_cols = jnp.stack([interior[..., 0], interior[..., -1]], -1)
    beside = with_halo(side_cols, (("lon", 3),), 1, True)
    result = interior[..., 1:-1]
    result = result.at[..., 0].add(beside[..., 0])
    result = result.at[..., -1].add(beside[..., -1])
    return result


def per_device(fields, weight_one, weight_two, edge_flips, cotangent):
    tile_rows, tile_cols = (fields.shape[2], fields.shape[3])
    edge_info = edge_flags(edge_flips)
    patch_in = patches_of(padded(fields, edge_info), tile_rows, tile_cols)
    hidden = convolve(patch_in, weight_one)
    activation = jax.nn.silu(hidden).astype(jnp.bfloat16)
    patch_act = patches_of(padded(activation, edge_info), tile_rows, tile_cols)
    output = (fields.astype(jnp.float32) + convolve(patch_act, weight_two)).astype(jnp.bfloat16)
    local_two = jnp.einsum(
        "bohw,btchw->toc", cotangent, patch_act, preferred_element_type=jnp.float32
    )
    back_act = returned(transposed(cotangent, weight_two, tile_rows, tile_cols), edge_info)
    sigmoid_h = jax.nn.sigmoid(hidden)
    back_hidden = (back_act * sigmoid_h * (1.0 + hidden * (1.0 - sigmoid_h))).astype(jnp.bfloat16)
    local_one = jnp.einsum(
        "bohw,btchw->toc", back_hidden, patch_in, preferred_element_type=jnp.float32
    )
    grad_one, grad_two = lax.psum((local_one, local_two), ("lon", "lat", "dp"))
    back_fields = returned(transposed(back_hidden, weight_one, tile_rows, tile_cols), edge_info)
    grad_fields = (cotangent.astype(jnp.float32) + back_fields).astype(jnp.bfloat16)
    return (output, grad_fields, grad_one, grad_two)


def solution(mesh):
    in_specs = (P("dp", None, "lat", "lon"), P(), P(), P(), P("dp", None, "lat", "lon"))
    out_specs = (P("dp", None, "lat", "lon"), P("dp", None, "lat", "lon"), P(), P())
    return jax.shard_map(
        per_device, mesh=mesh, in_specs=in_specs, out_specs=out_specs, check_vma=False
    )
```

profile of v0, /device:TPU:0, one launch (start us, length us, event | category | flops | bytes accessed | tf_op | source)
XLA Modules:
  0.0 317.7 jit_solution(13688654124079831977)
XLA Ops:
  7.2 1.4 copy.9
  8.6 3.1 collective-permute-start
  11.7 2.1 collective-permute-start.1
  15.0 1.4 and_reduce_fusion
  17.8 2.5 fusion.20
  20.3 4.0 %scatter-add.89 = f32[1,256,10,130]{1,3,2,0:T(8,128)S(1)} dynamic-update-slice(f32[1,256,10,130]{1,3,2,0:T(8,128)S(1)} %scatter-add.86, f32[1,256,8,128]{1,3,2,0:T(8,128)S(1)} %fusion.20, s32[]{:T(128)} %constant.652.clone.1, s32[]{:T(128)} %constant.652.clone.1, s32[]{:T(128)} %bitcast.50, s32[]{:T(128)} %bitcast.51) | dynamic-update-slice | bytes 2097156 | tf_op jit(solution)/shard_map/scatter-add | solution.py:81
  24.4 3.2 %add_select_fusion.1 = f32[1,256,8,128]{1,3,2,0:T(8,128)S(1)} fusion(f32[1,256,10,130]{1,3,2,0:T(8,128)S(1)} %scatter-add.89, s32[]{:T(128)} %bitcast.56, s32[]{:T(128)} %bitcast.57, pred[]{:T(512)} %and_reduce_fusion, bf16[9,256,256]{2,1,0:T(8,128)(2,1)} %param.59, bf16[256,8,128]{2,1,0:T(8,128)(2,1)S(1)} %bitcast.404), kind=kOutput, calls=%fused_computation.11 | convolution fusion | flops 134742016 | bytes 2754048 | tf_op jit(solution)/shard_map/oc,bohw->bchw/dot_general | solution.py:73
  27.6 4.0 %scatter-add.90 = f32[1,256,10,130]{1,3,2,0:T(8,128)S(1)} dynamic-update-slice(f32[1,256,10,130]{1,3,2,0:T(8,128)S(1)} %scatter-add.89, f32[1,256,8,128]{1,3,2,0:T(8,128)S(1)} %add_select_fusion.1, s32[]{:T(128)} %constant.652.clone.1, s32[]{:T(128)} %constant.652.clone.1, s32[]{:T(128)} %bitcast.56, s32[]{:T(128)} %bitcast.57) | dynamic-update-slice | bytes 2097156 | tf_op jit(solution)/shard_map/scatter-add | solution.py:81
  34.1 2.7 scatter-add.94
  38.1 2.7 scatter-add.95
  43.4 2.7 scatter-add.99
  47.4 2.7 scatter-add.100
  51.4 1.7 collective-permute-start.3
  55.1 4.6 %collective-permute-start.8 = (f32[1,256,1,130]{1,3,2,0:T(8,128)S(1)}, f32[1,256,1,130]{1,3,2,0:T(8,128)S(1)}, u32[]{:S(2)}, u32[]{:S(2)}) collective-permute-start(f32[1,256,1,130]{1,3,2,0:T(8,128)S(1)} %get-tuple-element.327), channel_id=1, source_target_pairs={{0,4},{1,5},{2,6},{3,7},{8,12},{9,13},{10,14},{11,15},{16,20},{17,... | collective-permute-start | bytes 399368 | tf_op jit(solution)/shard_map/ppermute | solution.py:15
  61.1 3.9 %collective-permute-done.2 = bf16[1,256,1,130]{1,3,2,0:T(8,128)(2,1)S(1)} collective-permute-done((bf16[1,256,1,130]{1,3,2,0:T(8,128)(2,1)S(1)}, bf16[1,256,1,130]{1,3,2,0:T(8,128)(2,1)S(1)}, u32[]{:S(2)}, u32[]{:S(2)}) %collective-permute-start.2) | collective-permute-done | bytes 66592 | tf_op jit(solution)/shard_map/ppermute | solution.py:15
  68.9 2.1 copy-done.8
  72.1 3.8 %collective-permute-start.11 = (f32[1,256,8,1]{1,3,2,0:T(1,128)S(1)}, f32[1,256,8,1]{1,3,2,0:T(1,128)S(1)}, u32[]{:S(2)}, u32[]{:S(2)}) collective-permute-start(f32[1,256,8,1]{1,3,2,0:T(1,128)S(1)} %get-tuple-element.332), channel_id=1, source_target_pairs={{8,0},{16,8},{24,16},{0,24},{9,1},{17,9},{25,17},{1,25},{10,2},{18... | collective-permute-start | bytes 24584 | tf_op jit(solution)/shard_map/ppermute | solution.py:17
  75.9 1.5 scatter-add.105
  78.3 1.5 scatter-add.106
  79.8 4.4 %multiply_convert_fusion = (bf16[1,256,8,128]{1,3,2,0:T(8,128)(2,1)S(1)}, bf16[1,256,8,128]{1,3,2,0:T(8,128)(2,1)S(1)}) fusion(f32[1,256,8,128]{1,3,2,0:T(8,128)} %scatter-add.106, bf16[9,256,256]{2,1,0:T(8,128)(2,1)S(1)} %copy-done.5, bf16[1,9,256,8,128]{2,4,1,3,0:T(8,128)(2,1)} %copy-done.8), kind=kOutput, calls=%fused_computation.55 | convolution fusion | flops 1210843136 | bytes 7995392 | tf_op jit(solution)/shard_map/toc,btchw->bohw/dot_general | solution.py:65
  84.2 2.9 fusion.8
  87.4 2.6 fusion.29
  90.2 4.2 %collective-permute-start.5 = (bf16[1,256,8,1]{1,3,2,0:T(2,128)(2,1)S(1)}, bf16[1,256,8,1]{1,3,2,0:T(2,128)(2,1)S(1)}, u32[]{:S(2)}, u32[]{:S(2)}) collective-permute-start(bf16[1,256,8,1]{1,3,2,0:T(2,128)(2,1)S(1)} %get-tuple-element.345), channel_id=1, source_target_pairs={{8,0},{16,8},{24,16},{0,24},{9,1},{17,9},{25,17},{1,25},{10,2},{18... | collective-permute-start | bytes 12296 | tf_op jit(solution)/shard_map/ppermute | solution.py:17
  94.3 7.2 %scatter-add.110 = f32[1,256,10,130]{1,3,2,0:T(8,128)S(1)} dynamic-update-slice(f32[1,256,10,130]{1,3,2,0:T(8,128)S(1)} %scatter-add.109, f32[1,256,8,128]{1,3,2,0:T(8,128)} %fusion.29, s32[]{:T(128)} %constant.652.clone.1, s32[]{:T(128)} %constant.652.clone.1, s32[]{:T(128)} %bitcast.50, s32[]{:T(128)} %bitcast.51) | dynamic-update-slice | bytes 2097156 | tf_op jit(solution)/shard_map/scatter-add | solution.py:81
  101.5 4.1 %add_select_fusion = f32[1,256,8,128]{1,3,2,0:T(8,128)} fusion(f32[1,256,10,130]{1,3,2,0:T(8,128)S(1)} %scatter-add.110, s32[]{:T(128)} %bitcast.56, s32[]{:T(128)} %bitcast.57, bf16[1,256,8,128]{1,3,2,0:T(8,128)(2,1)S(1)} %get-tuple-element.334, pred[]{:T(512)} %and_reduce_fusion, bf16[9,256,256]{2,1,0:T(8,128)(2,1)} %param.58), kind=kOutput, calls=%fused_computation.10 | convolution fusion | flops 134742016 | bytes 2754048 | tf_op jit(solution)/shard_map/oc,bohw->bchw/dot_general | solution.py:73
  105.7 7.2 %scatter-add.111 = f32[1,256,10,130]{1,3,2,0:T(8,128)S(1)} dynamic-update-slice(f32[1,256,10,130]{1,3,2,0:T(8,128)S(1)} %scatter-add.110, f32[1,256,8,128]{1,3,2,0:T(8,128)} %add_select_fusion, s32[]{:T(128)} %constant.652.clone.1, s32[]{:T(128)} %constant.652.clone.1, s32[]{:T(128)} %bitcast.56, s32[]{:T(128)} %bitcast.57) | dynamic-update-slice | bytes 2097156 | tf_op jit(solution)/shard_map/scatter-add | solution.py:81
  114.1 2.2 fusion.32
  116.3 5.9 %scatter-add.115 = f32[1,256,10,130]{1,3,2,0:T(8,128)S(1)} dynamic-update-slice(f32[1,256,10,130]{1,3,2,0:T(8,128)S(1)} %fusion.31, f32[1,256,8,128]{1,3,2,0:T(8,128)} %fusion.32, s32[]{:T(128)} %constant.652.clone.1, s32[]{:T(128)} %constant.652.clone.1, s32[]{:T(128)} %constant.659.clone.1, s32[]{:T(128)} %constant.659.clone.1) | dynamic-update-slice | bytes 2097156 | tf_op jit(solution)/shard_map/scatter-add | solution.py:81
  122.1 2.2 fusion.33
  124.3 5.9 %scatter-add.116 = f32[1,256,10,130]{1,3,2,0:T(8,128)S(1)} dynamic-update-slice(f32[1,256,10,130]{1,3,2,0:T(8,128)S(1)} %scatter-add.115, f32[1,256,8,128]{1,3,2,0:T(8,128)} %fusion.33, s32[]{:T(128)} %constant.652.clone.1, s32[]{:T(128)} %constant.652.clone.1, s32[]{:T(128)} %constant.659.clone.1, s32[]{:T(128)} %constant.663.clone.1) | dynamic-update-slice | bytes 2097156 | tf_op jit(solution)/shard_map/scatter-add | solution.py:81
  131.4 2.2 fusion.36
  133.6 5.9 %scatter-add.120 = f32[1,256,10,130]{1,3,2,0:T(8,128)S(1)} dynamic-update-slice(f32[1,256,10,130]{1,3,2,0:T(8,128)S(1)} %fusion.35, f32[1,256,8,128]{1,3,2,0:T(8,128)} %fusion.36, s32[]{:T(128)} %constant.652.clone.1, s32[]{:T(128)} %constant.652.clone.1, s32[]{:T(128)} %constant.663.clone.1, s32[]{:T(128)} %constant.659.clone.1) | dynamic-update-slice | bytes 2097156 | tf_op jit(solution)/shard_map/scatter-add | solution.py:81
  140.7 2.2 fusion.37
  142.8 5.9 %scatter-add.121 = f32[1,256,10,130]{1,3,2,0:T(8,128)S(1)} dynamic-update-slice(f32[1,256,10,130]{1,3,2,0:T(8,128)S(1)} %scatter-add.120, f32[1,256,8,128]{1,3,2,0:T(8,128)} %fusion.37, s32[]{:T(128)} %constant.652.clone.1, s32[]{:T(128)} %constant.652.clone.1, s32[]{:T(128)} %constant.663.clone.1, s32[]{:T(128)} %constant.663.clone.1) | dynamic-update-slice | bytes 2097156 | tf_op jit(solution)/shard_map/scatter-add | solution.py:81
  148.7 1.6 collective-permute-start.6
  151.5 1.6 collective-permute-done.6
  153.5 1.5 select_bitcast_fusion.4
  156.7 2.1 copy-done.10
  158.9 2.9 fusion.11
  163.1 2.6 collective-permute-start.12
  166.1 1.4 collective-permute-start.13
  167.5 3.2 %collective-permute-done.12 = f32[1,256,1,130]{1,3,2,0:T(8,128)S(1)} collective-permute-done((f32[1,256,1,130]{1,3,2,0:T(8,128)S(1)}, f32[1,256,1,130]{1,3,2,0:T(8,128)S(1)}, u32[]{:S(2)}, u32[]{:S(2)}) %collective-permute-start.12) | collective-permute-done | bytes 133152 | tf_op jit(solution)/shard_map/ppermute | solution.py:15
  170.7 4.4 %collective-permute-done.13 = f32[1,256,1,130]{1,3,2,0:T(8,128)S(1)} collective-permute-done((f32[1,256,1,130]{1,3,2,0:T(8,128)S(1)}, f32[1,256,1,130]{1,3,2,0:T(8,128)S(1)}, u32[]{:S(2)}, u32[]{:S(2)}) %collective-permute-start.13) | collective-permute-done | bytes 133152 | tf_op jit(solution)/shard_map/ppermute | solution.py:17
  176.2 3.9 %fusion.41 = bf16[1,256,8,128]{1,3,2,0:T(8,128)(2,1)S(1)} fusion(bf16[1,9,256,8,128]{2,4,3,1,0:T(8,128)(2,1)} %copy-done.10, bf16[9,256,256]{2,1,0:T(8,128)(2,1)S(1)} %copy-done.6, bf16[1,256,8,128]{1,3,2,0:T(8,128)(2,1)S(1)} %copy.9), kind=kOutput, calls=%fused_computation.51 | convolution fusion | flops 1208745984 | bytes 6946816 | tf_op jit(solution)/shard_map/toc,btchw->bohw/dot_general | solution.py:65
  181.3 3.9 %collective-permute-start.15 = (f32[1,256,8,1]{1,3,2,0:T(1,128)S(1)}, f32[1,256,8,1]{1,3,2,0:T(1,128)S(1)}, u32[]{:S(2)}, u32[]{:S(2)}) collective-permute-start(f32[1,256,8,1]{1,3,2,0:T(1,128)S(1)} %get-tuple-element.330), channel_id=1, source_target_pairs={{8,0},{16,8},{24,16},{0,24},{9,1},{17,9},{25,17},{1,25},{10,2},{18... | collective-permute-start | bytes 24584 | tf_op jit(solution)/shard_map/ppermute | solution.py:17
  187.9 117.8 %all-reduce.5.cloned.1.call-done = (f32[9,256,256]{1,2,0:T(8,128)}, f32[9,256,256]{1,2,0:T(8,128)}) async-done(((f32[9,256,256]{1,2,0:T(8,128)}, f32[9,256,256]{1,2,0:T(8,128)}), (f32[9,256,256]{1,2,0:T(8,128)}, f32[9,256,256]{1,2,0:T(8,128)})) %all-reduce.5.cloned.1.call-update) | async-done | bytes 4718608 | tf_op jit(solution)/shard_map/psum | solution.py:119
  305.7 3.2 %copy.38 = f32[9,256,256]{2,1,0:T(8,128)} copy(f32[9,256,256]{1,2,0:T(8,128)} %get-tuple-element.320) | data formatting | bytes 4718592
  308.9 1.9 copy.39
  (122 shorter events, 34.5 us)
Async XLA Ops:
  7.2 9.3 %copy-start = (bf16[1,256,8,128]{3,2,1,0:T(8,128)(2,1)S(1)}, bf16[1,256,8,128]{3,2,1,0:T(8,128)(2,1)}, u32[]{:S(2)}) copy-start(bf16[1,256,8,128]{3,2,1,0:T(8,128)(2,1)} %param.61) | copy-start | bytes 1572868
  7.2 298.5 %all-reduce.5.cloned.1.call-start = ((), (), s32[]{:S(2)}) async-start(), calls=%async_computation | async-start | bytes 9437184 | tf_op jit(solution)/shard_map/psum | solution.py:119
  8.6 42.8 %collective-permute-start = (bf16[1,256,8,1]{1,3,2,0:T(2,128)(2,1)S(1)}, bf16[1,256,8,1]{1,3,2,0:T(2,128)(2,1)S(1)}, u32[]{:S(2)}, u32[]{:S(2)}) collective-permute-start(bf16[1,256,8,1]{1,3,2,0:T(2,128)(2,1)S(1)} %get-tuple-element.346), channel_id=1, source_target_pairs={{0,8},{8,16},{16,24},{24,0},{1,9},{9,17},{17,25},{25,1},{2,10},{10... | collective-permute-start | bytes 12296 | tf_op jit(solution)/shard_map/ppermute | solution.py:15
  11.7 39.7 %collective-permute-start.1 = (bf16[1,256,8,1]{1,3,2,0:T(2,128)(2,1)S(1)}, bf16[1,256,8,1]{1,3,2,0:T(2,128)(2,1)S(1)}, u32[]{:S(2)}, u32[]{:S(2)}) collective-permute-start(bf16[1,256,8,1]{1,3,2,0:T(2,128)(2,1)S(1)} %get-tuple-element.347), channel_id=1, source_target_pairs={{8,0},{16,8},{24,16},{0,24},{9,1},{17,9},{25,17},{1,25},{10,2},{18... | collective-permute-start | bytes 12296 | tf_op jit(solution)/shard_map/ppermute | solution.py:17
  47.4 3.4 %copy-start.11 = (s32[1,4]{1,0:T(1,128)S(1)}, s32[1,4]{1,0:T(1,128)}, u32[]{:S(2)}) copy-start(s32[1,4]{1,0:T(1,128)} %param.60) | copy-start | bytes 52
  51.4 9.3 %collective-permute-start.3 = (bf16[1,256,1,130]{1,3,2,0:T(8,128)(2,1)S(1)}, bf16[1,256,1,130]{1,3,2,0:T(8,128)(2,1)S(1)}, u32[]{:S(2)}, u32[]{:S(2)}) collective-permute-start(bf16[1,256,1,130]{1,3,2,0:T(8,128)(2,1)S(1)} %get-tuple-element.342), channel_id=1, source_target_pairs={{4,0},{0,4},{5,1},{1,5},{6,2},{2,6},{7,3},{3,7},{12,8},{8,12},{13,... | collective-permute-start | bytes 199688 | tf_op jit(solution)/shard_map/ppermute | solution.py:17
  53.8 14.8 %collective-permute-start.9 = (f32[1,256,1,130]{1,3,2,0:T(8,128)S(1)}, f32[1,256,1,130]{1,3,2,0:T(8,128)S(1)}, u32[]{:S(2)}, u32[]{:S(2)}) collective-permute-start(f32[1,256,1,130]{1,3,2,0:T(8,128)S(1)} %get-tuple-element.326), channel_id=1, source_target_pairs={{4,0},{5,1},{6,2},{7,3},{12,8},{13,9},{14,10},{15,11},{20,16},{21,... | collective-permute-start | bytes 399368 | tf_op jit(solution)/shard_map/ppermute | solution.py:17
  55.1 12.6 %collective-permute-start.8 = (f32[1,256,1,130]{1,3,2,0:T(8,128)S(1)}, f32[1,256,1,130]{1,3,2,0:T(8,128)S(1)}, u32[]{:S(2)}, u32[]{:S(2)}) collective-permute-start(f32[1,256,1,130]{1,3,2,0:T(8,128)S(1)} %get-tuple-element.327), channel_id=1, source_target_pairs={{0,4},{1,5},{2,6},{3,7},{8,12},{9,13},{10,14},{11,15},{16,20},{17,... | collective-permute-start | bytes 399368 | tf_op jit(solution)/shard_map/ppermute | solution.py:15
  60.7 4.3 %collective-permute-start.2 = (bf16[1,256,1,130]{1,3,2,0:T(8,128)(2,1)S(1)}, bf16[1,256,1,130]{1,3,2,0:T(8,128)(2,1)S(1)}, u32[]{:S(2)}, u32[]{:S(2)}) collective-permute-start(bf16[1,256,1,130]{1,3,2,0:T(8,128)(2,1)S(1)} %get-tuple-element.343), channel_id=1, source_target_pairs={{0,4},{4,0},{1,5},{5,1},{2,6},{6,2},{3,7},{7,3},{8,12},{12,8},{9,1... | collective-permute-start | bytes 199688 | tf_op jit(solution)/shard_map/ppermute | solution.py:15
  67.3 1.3 copy-start.1
  68.7 11.1 %copy-start.5 = (bf16[9,256,256]{2,1,0:T(8,128)(2,1)S(1)}, bf16[9,256,256]{2,1,0:T(8,128)(2,1)}, u32[]{:S(2)}) copy-start(bf16[9,256,256]{2,1,0:T(8,128)(2,1)} %param.58) | copy-start | bytes 3538948
  68.7 7.2 %collective-permute-start.10 = (f32[1,256,8,1]{1,3,2,0:T(1,128)S(1)}, f32[1,256,8,1]{1,3,2,0:T(1,128)S(1)}, u32[]{:S(2)}, u32[]{:S(2)}) collective-permute-start(f32[1,256,8,1]{1,3,2,0:T(1,128)S(1)} %get-tuple-element.333), channel_id=1, source_target_pairs={{0,8},{8,16},{16,24},{24,0},{1,9},{9,17},{17,25},{25,1},{2,10},{10... | collective-permute-start | bytes 24584 | tf_op jit(solution)/shard_map/ppermute | solution.py:15
  68.9 2.1 copy-start.8
  72.1 5.3 %collective-permute-start.11 = (f32[1,256,8,1]{1,3,2,0:T(1,128)S(1)}, f32[1,256,8,1]{1,3,2,0:T(1,128)S(1)}, u32[]{:S(2)}, u32[]{:S(2)}) collective-permute-start(f32[1,256,8,1]{1,3,2,0:T(1,128)S(1)} %get-tuple-element.332), channel_id=1, source_target_pairs={{8,0},{16,8},{24,16},{0,24},{9,1},{17,9},{25,17},{1,25},{10,2},{18... | collective-permute-start | bytes 24584 | tf_op jit(solution)/shard_map/ppermute | solution.py:17
  79.8 4.4 %copy-start.9 = (bf16[1,9,256,8,128]{2,4,1,3,0:T(8,128)(2,1)S(1)}, bf16[1,9,256,8,128]{2,4,1,3,0:T(8,128)(2,1)}, u32[]{:S(2)}) copy-start(bf16[1,9,256,8,128]{2,4,1,3,0:T(8,128)(2,1)} %copy-done.8) | copy-start | bytes 14155780
  90.1 49.3 %collective-permute-start.4 = (bf16[1,256,8,1]{1,3,2,0:T(2,128)(2,1)S(1)}, bf16[1,256,8,1]{1,3,2,0:T(2,128)(2,1)S(1)}, u32[]{:S(2)}, u32[]{:S(2)}) collective-permute-start(bf16[1,256,8,1]{1,3,2,0:T(2,128)(2,1)S(1)} %get-tuple-element.344), channel_id=1, source_target_pairs={{0,8},{8,16},{16,24},{24,0},{1,9},{9,17},{17,25},{25,1},{2,10},{10... | collective-permute-start | bytes 12296 | tf_op jit(solution)/shard_map/ppermute | solution.py:15
  90.2 49.3 %collective-permute-start.5 = (bf16[1,256,8,1]{1,3,2,0:T(2,128)(2,1)S(1)}, bf16[1,256,8,1]{1,3,2,0:T(2,128)(2,1)S(1)}, u32[]{:S(2)}, u32[]{:S(2)}) collective-permute-start(bf16[1,256,8,1]{1,3,2,0:T(2,128)(2,1)S(1)} %get-tuple-element.345), channel_id=1, source_target_pairs={{8,0},{16,8},{24,16},{0,24},{9,1},{17,9},{25,17},{1,25},{10,2},{18... | collective-permute-start | bytes 12296 | tf_op jit(solution)/shard_map/ppermute | solution.py:17
  140.2 10.2 %collective-permute-start.7 = (bf16[1,256,1,130]{1,3,2,0:T(8,128)(2,1)}, bf16[1,256,1,130]{1,3,2,0:T(8,128)(2,1)}, u32[]{:S(2)}, u32[]{:S(2)}) collective-permute-start(bf16[1,256,1,130]{1,3,2,0:T(8,128)(2,1)} %get-tuple-element.338), channel_id=1, source_target_pairs={{4,0},{0,4},{5,1},{1,5},{6,2},{2,6},{7,3},{3,7},{12,8},{8,12},{13,... | collective-permute-start | bytes 199688 | tf_op jit(solution)/shard_map/ppermute | solution.py:17
  142.8 5.9 %copy-start.7 = (bf16[1,256,1,130]{1,3,2,0:T(8,128)(2,1)S(1)}, bf16[1,256,1,130]{1,3,2,0:T(8,128)(2,1)}, u32[]{:S(2)}) copy-start(bf16[1,256,1,130]{1,3,2,0:T(8,128)(2,1)} %get-tuple-element.339) | copy-start | bytes 199684
  148.7 4.4 %collective-permute-start.6 = (bf16[1,256,1,130]{1,3,2,0:T(8,128)(2,1)S(1)}, bf16[1,256,1,130]{1,3,2,0:T(8,128)(2,1)S(1)}, u32[]{:S(2)}, u32[]{:S(2)}) collective-permute-start(bf16[1,256,1,130]{1,3,2,0:T(8,128)(2,1)S(1)} %copy-done.7), channel_id=1, source_target_pairs={{0,4},{4,0},{1,5},{5,1},{2,6},{6,2},{3,7},{7,3},{8,12},{12,8},{9,1... | collective-permute-start | bytes 199688 | tf_op jit(solution)/shard_map/ppermute | solution.py:15
  156.7 2.1 copy-start.10
  163.1 7.7 %collective-permute-start.12 = (f32[1,256,1,130]{1,3,2,0:T(8,128)S(1)}, f32[1,256,1,130]{1,3,2,0:T(8,128)S(1)}, u32[]{:S(2)}, u32[]{:S(2)}) collective-permute-start(f32[1,256,1,130]{1,3,2,0:T(8,128)S(1)} %get-tuple-element.323), channel_id=1, source_target_pairs={{0,4},{1,5},{2,6},{3,7},{8,12},{9,13},{10,14},{11,15},{16,20},{17,... | collective-permute-start | bytes 399368 | tf_op jit(solution)/shard_map/ppermute | solution.py:15
  166.0 10.3 %copy-start.6 = (bf16[9,256,256]{2,1,0:T(8,128)(2,1)S(1)}, bf16[9,256,256]{2,1,0:T(8,128)(2,1)}, u32[]{:S(2)}) copy-start(bf16[9,256,256]{2,1,0:T(8,128)(2,1)} %param.59) | copy-start | bytes 3538948
  166.1 9.1 %collective-permute-start.13 = (f32[1,256,1,130]{1,3,2,0:T(8,128)S(1)}, f32[1,256,1,130]{1,3,2,0:T(8,128)S(1)}, u32[]{:S(2)}, u32[]{:S(2)}) collective-permute-start(f32[1,256,1,130]{1,3,2,0:T(8,128)S(1)} %get-tuple-element.322), channel_id=1, source_target_pairs={{4,0},{5,1},{6,2},{7,3},{12,8},{13,9},{14,10},{15,11},{20,16},{21,... | collective-permute-start | bytes 399368 | tf_op jit(solution)/shard_map/ppermute | solution.py:17
  175.1 1.0 copy-start.2
  176.1 9.1 %collective-permute-start.14 = (f32[1,256,8,1]{1,3,2,0:T(1,128)S(1)}, f32[1,256,8,1]{1,3,2,0:T(1,128)S(1)}, u32[]{:S(2)}, u32[]{:S(2)}) collective-permute-start(f32[1,256,8,1]{1,3,2,0:T(1,128)S(1)} %get-tuple-element.331), channel_id=1, source_target_pairs={{0,8},{8,16},{16,24},{24,0},{1,9},{9,17},{17,25},{25,1},{2,10},{10... | collective-permute-start | bytes 24584 | tf_op jit(solution)/shard_map/ppermute | solution.py:15
  176.2 5.0 %copy-start.3 = (f32[1,256,8,130]{1,3,2,0:T(8,128)S(1)}, f32[1,256,8,130]{1,3,2,0:T(8,128)}, u32[]{:S(2)}) copy-start(f32[1,256,8,130]{1,3,2,0:T(8,128)} %copy-done.2) | copy-start | bytes 3194884
  181.3 5.3 %collective-permute-start.15 = (f32[1,256,8,1]{1,3,2,0:T(1,128)S(1)}, f32[1,256,8,1]{1,3,2,0:T(1,128)S(1)}, u32[]{:S(2)}, u32[]{:S(2)}) collective-permute-start(f32[1,256,8,1]{1,3,2,0:T(1,128)S(1)} %get-tuple-element.330), channel_id=1, source_target_pairs={{8,0},{16,8},{24,16},{0,24},{9,1},{17,9},{25,17},{1,25},{10,2},{18... | collective-permute-start | bytes 24584 | tf_op jit(solution)/shard_map/ppermute | solution.py:17
  305.7 3.2 %copy-start.4 = (f32[9,256,256]{1,2,0:T(8,128)S(1)}, f32[9,256,256]{1,2,0:T(8,128)}, u32[]{:S(2)}) copy-start(f32[9,256,256]{1,2,0:T(8,128)} %get-tuple-element.321) | copy-start | bytes 7077892
Sparse Core Ops, SparseCore 0:
  161.9 143.7 all-reduce.4
where the time goes:
time: 319 us; the launch traced here: 318 us
  waiting for transfers between devices  132 us (41%)
  local copies, waits for them, and re-layouts  82.7 us (26%)
  matrix products  46.7 us (15%)
  starting transfers between devices  30.9 us (10%)
  between operations  14.8 us (5%)
  other arithmetic  10.4 us (3%)
    psum x1, waiting for transfers between devices, per_device(): grad_one, grad_two = lax.psum((local_one, local_two), ('lon', 'lat', 'dp'))  118 us
    scatter-add x14, local copies, waits for them, and re-layouts, transposed(): padded_grad = padded_grad.at[:, :, tap_row:tap_row + tile_rows, tap_col:t...  57 us
    dot_general x18, matrix products, transposed(): jnp.einsum('oc,bohw->bchw', weight[3 * tap_row + tap_col], grad_tile, pre...  32.6 us
    ppermute x8, starting transfers between devices, with_halo(): lax.ppermute(head, axis, [((i + 1) % count, i) for i in range(ends)])  18.9 us
    unnamed x42, local copies, waits for them, and re-layouts  16.2 us
    ppermute x8, starting transfers between devices, with_halo(): lax.ppermute(tail, axis, [(i, (i + 1) % count) for i in range(ends)])  12 us
    ppermute x8, waiting for transfers between devices, with_halo(): lax.ppermute(tail, axis, [(i, (i + 1) % count) for i in range(ends)])  8.72 us
    dot_general x2, matrix products, convolve(): jnp.einsum('toc,btchw->bohw', weight, patches, preferred_element_type=jnp...  8.27 us
  transfers between devices with their start and end apart: 17, of which 6 were waited for; matrix products, arithmetic and copies ran while one was open for 34% of the time, Pallas kernels for 0%

commit v1 on v0

v1 whole, which is shorter than its diff:
```python
import functools

import jax
import jax.numpy as jnp
from jax import lax
from jax.experimental import pallas as pl
from jax.experimental.pallas import tpu as pltpu
from jax.sharding import PartitionSpec as P

F32 = jnp.float32
BF16 = jnp.bfloat16
NN = (((1,), (0,)), ((), ()))
NT = (((1,), (1,)), ((), ()))
SIDES = ("W", "E", "U", "D", "UW", "UE", "DW", "DE")


def product(a, b, dims):
    return lax.dot_general(a, b, dims, preferred_element_type=F32)


def kernel(
    sizes,
    x_ref, g_ref, w1_ref, w2_ref, flip_ref,
    out_ref, gf_ref, o1_ref, o2_ref,
    x1, x2, gz, bz, gt, bt, q, hid, act,
    cell_out, cell_in, row_out, row_in,
    s0, a0, r0, s1, a1, r1, s2, a2, r2, near,
    halo_send, halo_recv, sum_send, sum_recv,
):
    n_lon, n_lat, n_dp, rows, cols, ch = sizes
    cells = rows * cols
    ny = n_dp // 2
    lon, lat, dp = lax.axis_index("lon"), lax.axis_index("lat"), lax.axis_index("dp")
    core, y = lax.rem(dp, 2), lax.div(dp, 2)
    west, east = lax.rem(lon + n_lon - 1, n_lon), lax.rem(lon + 1, n_lon)
    has_up, has_down = lat > 0, lat < n_lat - 1
    up, down = jnp.maximum(lat - 1, 0), jnp.minimum(lat + 1, n_lat - 1)

    cell_in[...] = jnp.zeros_like(cell_in)
    cell_out[...] = jnp.zeros_like(cell_out)
    row_in[...] = jnp.zeros_like(row_in)
    barrier = pltpu.get_barrier_semaphore()
    greeted = 0
    for i in range(n_lon):
        for j in range(n_lat):
            if i or j:
                pl.semaphore_signal(
                    barrier, inc=1,
                    device_id={"lon": lax.rem(lon + i, n_lon), "lat": lax.rem(lat + j, n_lat), "dp": dp},
                    device_id_type=pl.DeviceIdType.MESH,
                )
                greeted += 1
    for k in range(1, n_dp):
        pl.semaphore_signal(
            barrier, inc=1,
            device_id={"lon": lon, "lat": lat, "dp": lax.rem(dp + k, n_dp)},
            device_id_type=pl.DeviceIdType.MESH,
        )
        greeted += 1

    def remote(src, dst, send, recv, to_lon, to_lat, to_dp):
        return pltpu.make_async_remote_copy(
            src_ref=src, dst_ref=dst, send_sem=send, recv_sem=recv,
            device_id={"lon": to_lon, "lat": to_lat, "dp": to_dp},
            device_id_type=pl.DeviceIdType.MESH,
        )

    opposite = {"W": "E", "E": "W", "U": "D", "D": "U", "UW": "DE", "UE": "DW", "DW": "UE", "DE": "UW"}

    def halo_copy(e, side):
        to_lon = west if "W" in side else east if "E" in side else lon
        to_lat = up if "U" in side else down if "D" in side else lat
        slot, there = SIDES.index(side), SIDES.index(opposite[side])
        if side in ("U", "D"):
            src, dst = row_out.at[e, slot - 2], row_in.at[e, there - 2]
        else:
            src, dst = cell_out.at[e, slot], cell_in.at[e, there]
        return remote(src, dst, halo_send.at[e, slot], halo_recv.at[e, there], to_lon, to_lat, dp)

    def guarded(side, action):
        if "U" in side:
            pl.when(has_up)(action)
        elif "D" in side:
            pl.when(has_down)(action)
        else:
            action()

    def halo_start(e):
        for side in ("U", "D", "W", "E", "UW", "UE", "DW", "DE"):
            copy = halo_copy(e, side)
            guarded(side, copy.start)

    def halo_wait(e):
        for side in SIDES:
            copy = halo_copy(e, side)
            guarded(side, copy.wait_send)
            guarded(opposite[side], copy.wait_recv)

    line = lax.broadcasted_iota(jnp.int32, (cols, ch), 0)
    ja = lax.broadcasted_iota(jnp.int32, (cols, cols), 0)
    jb = lax.broadcasted_iota(jnp.int32, (cols, cols), 1)
    exchange = jnp.where(ja + jb == cols - 1, 1.0, 0.0).astype(BF16)
    flip_up, flip_down = flip_ref[0:1, :] > 0.5, flip_ref[8:9, :] > 0.5

    def turned(flag, west_cell, middle, east_cell):
        back = product(exchange, middle, NN)
        return (
            jnp.where(flag, east_cell, west_cell),
            jnp.where(flag, back, middle.astype(F32)),
            jnp.where(flag, west_cell, east_cell),
        )

    def send_field(e, ref):
        for h in range(rows):
            top = ref[h * cols : h * cols + 16, :].astype(F32)
            low = ref[(h + 1) * cols - 16 : (h + 1) * cols, :].astype(F32)
            cell_out[e, 0, h : h + 1, :] = top[0:1]
            cell_out[e, 1, h : h + 1, :] = low[15:16]
            if h == 0:
                cell_out[e, 4, 0:1, :] = top[0:1]
                cell_out[e, 5, 0:1, :] = low[15:16]
            if h == rows - 1:
                cell_out[e, 6, 0:1, :] = top[0:1]
                cell_out[e, 7, 0:1, :] = low[15:16]
        row_out[e, 0] = ref[0:cols, :]
        row_out[e, 1] = ref[cells - cols : cells, :]
        halo_start(e)

    def put_row(buf, i, west_cell, middle, east_cell):
        at = slice(i * cols, (i + 1) * cols)
        buf[at, 0:ch] = jnp.where(line == 0, west_cell, pltpu.roll(middle, 1, 0)).astype(BF16)
        buf[at, ch : 2 * ch] = middle.astype(BF16)
        buf[at, 2 * ch : 3 * ch] = jnp.where(
            line == cols - 1, east_cell, pltpu.roll(middle, cols - 1, 0)
        ).astype(BF16)

    def pad_field(e, ref, buf):
        halo_wait(e)
        for h in range(rows):
            put_row(
                buf, h + 1, cell_in[e, 0, h : h + 1, :],
                ref[h * cols : (h + 1) * cols, :].astype(F32), cell_in[e, 1, h : h + 1, :],
            )
        put_row(buf, 0, *turned(flip_up, cell_in[e, 4, 0:1, :], row_in[e, 0], cell_in[e, 5, 0:1, :]))
        put_row(buf, rows + 1, *turned(flip_down, cell_in[e, 6, 0:1, :], row_in[e, 1], cell_in[e, 7, 0:1, :]))

    block = cells // 2

    def conv(buf, w_ref, i):
        left = jnp.concatenate(
            [buf[i * block + r * cols : i * block + r * cols + block, :] for r in range(3)], 1
        )
        right = jnp.concatenate([w_ref[t] for t in range(9)], 1)
        return product(left, right, NT)

    def back_conv(e, z, w_ref):
        step = (rows + 2) // 2
        size = step * cols
        for i in range(2):
            left = jnp.concatenate(
                [z[i * size + (2 - r) * cols : i * size + (2 - r) * cols + size, :] for r in range(3)], 1
            )
            ys = [
                product(left, jnp.concatenate([w_ref[3 * r + s] for r in range(3)], 0), NN)
                for s in range(3)
            ]
            for k in range(step):
                n = i * step + k
                at = slice(k * cols, (k + 1) * cols)
                y0, y1, y2 = ys[0][at], ys[1][at], ys[2][at]
                total = (
                    y1
                    + jnp.where(line == cols - 1, 0.0, pltpu.roll(y0, cols - 1, 0))
                    + jnp.where(line == 0, 0.0, pltpu.roll(y2, 1, 0))
                )
                if 0 < n < rows + 1:
                    q[(n - 1) * cols : n * cols, :] = total
                    cell_out[e, 0, n - 1 : n, :] = y0[0:1]
                    cell_out[e, 1, n - 1 : n, :] = y2[cols - 1 : cols]
                else:
                    flag, slot = (flip_up, 0) if n == 0 else (flip_down, 1)
                    first, middle, last = turned(
                        flag, y0[0:1], total.astype(BF16), y2[cols - 1 : cols]
                    )
                    row_out[e, slot] = middle.astype(BF16)
                    cell_out[e, 4 + 2 * slot, 0:1, :] = first
                    cell_out[e, 5 + 2 * slot, 0:1, :] = last
        halo_start(e)

    def returned_row(e, h):
        value = q[h * cols : (h + 1) * cols, :]
        west_cell, east_cell = cell_in[e, 0, h : h + 1, :], cell_in[e, 1, h : h + 1, :]
        if h == 0:
            value = value + row_in[e, 0].astype(F32)
            west_cell = west_cell + cell_in[e, 4, 0:1, :]
            east_cell = east_cell + cell_in[e, 5, 0:1, :]
        if h == rows - 1:
            value = value + row_in[e, 1].astype(F32)
            west_cell = west_cell + cell_in[e, 6, 0:1, :]
            east_cell = east_cell + cell_in[e, 7, 0:1, :]
        return value + jnp.where(line == 0, west_cell, 0.0) + jnp.where(line == cols - 1, east_cell, 0.0)

    part_rows = 3 * ch
    half, quarter = part_rows // 2, part_rows // (2 * ny)
    piece = quarter // n_lat

    def start_all(copies):
        for copy in copies:
            copy.start()

    def finish(copies):
        for copy in copies:
            copy.wait()

    def gathered(p):
        ref = o1_ref if p < 3 else o2_ref
        return lambda start, size: ref.at[pl.ds(pl.multiple_of((p % 3) * part_rows + start, 16), size), :]

    core_at, y_at, lat_at = core * half, core * half + y * quarter, core * half + y * quarter + lat * piece
    slots = iter(range(1000))
    sem_core, sem_y, sem_lat, sem_lon, sem_lat2, sem_y2, sem_core2 = (
        [next(slots) for _ in range(n)] for n in (1, ny - 1, n_lat - 1, n_lon - 1, n_lat - 1, ny - 1, 1)
    )

    def to_core(p, src, dst, sem):
        return remote(src, dst, sum_send.at[p, sem], sum_recv.at[p, sem], lon, lat, y * 2 + 1 - core)

    def to_y(p, src, dst, sem, k):
        return remote(src, dst, sum_send.at[p, sem], sum_recv.at[p, sem], lon, lat, lax.rem(y + k, ny) * 2 + core)

    def to_lat(p, src, dst, sem, k):
        return remote(src, dst, sum_send.at[p, sem], sum_recv.at[p, sem], lon, lax.rem(lat + k, n_lat), dp)

    def to_lon(p, src, dst, sem, k):
        return remote(src, dst, sum_send.at[p, sem], sum_recv.at[p, sem], lax.rem(lon + k, n_lon), lat, dp)

    def rows_of(start, size):
        return pl.ds(pl.multiple_of(start, 16), size)

    def reduce_steps(p, grad):
        for s in range(3):
            a0[p, s * ch : (s + 1) * ch, :] = grad[:, s * ch : (s + 1) * ch]
            s0[p, s * ch : (s + 1) * ch, :] = grad[:, s * ch : (s + 1) * ch].astype(BF16)
        copies = [to_core(p, s0.at[p, rows_of((1 - core) * half, half), :], r0.at[p], sem_core[0])]
        start_all(copies)
        yield
        finish(copies)
        total = a0[p, rows_of(core_at, half), :] + r0[p].astype(F32)
        a1[p] = total
        s1[p] = total.astype(BF16)
        copies = [
            to_y(p, s1.at[p, rows_of(lax.rem(y + k, ny) * quarter, quarter), :], r1.at[p, k - 1], sem_y[k - 1], k)
            for k in range(1, ny)
        ]
        start_all(copies)
        yield
        finish(copies)
        total = a1[p, rows_of(y * quarter, quarter), :]
        for k in range(1, ny):
            total = total + r1[p, k - 1].astype(F32)
        a2[p] = total
        s2[p] = total.astype(BF16)
        copies = [
            to_lat(p, s2.at[p, rows_of(lax.rem(lat + k, n_lat) * piece, piece), :], r2.at[p, k - 1], sem_lat[k - 1], k)
            for k in range(1, n_lat)
        ]
        start_all(copies)
        yield
        finish(copies)
        total = a2[p, rows_of(lat * piece, piece), :]
        for k in range(1, n_lat):
            total = total + r2[p, k - 1].astype(F32)
        near[p, lon] = total.astype(BF16)
        copies = [to_lon(p, near.at[p, lon], near.at[p, lon], sem_lon[k - 1], k) for k in range(1, n_lon)]
        start_all(copies)
        yield
        finish(copies)
        total = near[p, 0].astype(F32)
        for k in range(1, n_lon):
            total = total + near[p, k].astype(F32)
        place = gathered(p)
        mine = place(lat_at, piece)
        mine[...] = total.astype(BF16)
        copies = [to_lat(p, mine, mine, sem_lat2[k - 1], k) for k in range(1, n_lat)]
        start_all(copies)
        yield
        finish(copies)
        mine = place(y_at, quarter)
        copies = [to_y(p, mine, mine, sem_y2[k - 1], k) for k in range(1, ny)]
        start_all(copies)
        yield
        finish(copies)
        mine = place(core_at, half)
        copies = [to_core(p, mine, mine, sem_core2[0])]
        start_all(copies)
        yield
        finish(copies)

    running = []

    def tick():
        for steps in list(running):
            if next(steps, "end") == "end":
                running.remove(steps)

    def begin(p, grad):
        tick()
        steps = reduce_steps(p, grad)
        next(steps)
        running.append(steps)

    pl.semaphore_wait(barrier, greeted)
    send_field(0, x_ref)

    edge = jnp.zeros((2 * cols, ch), BF16)
    for z in (gz, bz):
        z[0 : 2 * cols, :] = edge
        z[2 * cols + cells : 4 * cols + cells, :] = edge
    for h in range(rows):
        value = g_ref[h * cols : (h + 1) * cols, :]
        gz[(h + 2) * cols : (h + 3) * cols, :] = value
        gt[:, h * cols : (h + 1) * cols] = value.astype(F32).T.astype(BF16)
    back_conv(2, gz, w2_ref)

    pad_field(0, x_ref, x1)
    for i in range(2):
        value = conv(x1, w1_ref, i)
        hid[i * block : (i + 1) * block, :] = value
        act[i * block : (i + 1) * block, :] = (value / (1.0 + jnp.exp(-value))).astype(BF16)
    send_field(1, act)

    halo_wait(2)
    for h in range(rows):
        back = returned_row(2, h)
        value = hid[h * cols : (h + 1) * cols, :]
        sigma = 1.0 / (1.0 + jnp.exp(-value))
        back = back * sigma * (1.0 + value * (1.0 - sigma))
        bz[(h + 2) * cols : (h + 3) * cols, :] = back.astype(BF16)
        bt[:, h * cols : (h + 1) * cols] = back.T.astype(BF16)

    for r in range(3):
        begin(r, product(bt[...], x1[r * cols : r * cols + cells, :], NN))
    pad_field(1, act, x2)
    for r in range(3):
        begin(3 + r, product(gt[...], x2[r * cols : r * cols + cells, :], NN))
    back_conv(3, bz, w1_ref)
    tick()
    for i in range(2):
        at = slice(i * block, (i + 1) * block)
        out_ref[at, :] = (x_ref[at, :].astype(F32) + conv(x2, w2_ref, i)).astype(BF16)
        tick()
    halo_wait(3)
    for h in range(rows):
        at = slice(h * cols, (h + 1) * cols)
        gf_ref[at, :] = (g_ref[at, :].astype(F32) + returned_row(3, h)).astype(BF16)
    while running:
        tick()


def per_device(sizes, fields, weight_one, weight_two, edge_flips, cotangent):
    n_lon, n_lat, n_dp = sizes
    _, ch, rows, cols = fields.shape
    cells = rows * cols
    ny = n_dp // 2
    lat, lon = lax.axis_index("lat"), lax.axis_index("lon")
    upper = lax.dynamic_slice(edge_flips, (jnp.maximum(lat - 1, 0), lon), (1, 1))
    lower = lax.dynamic_slice(edge_flips, (jnp.minimum(lat, n_lat - 2), lon), (1, 1))
    flips = jnp.concatenate(
        [jnp.broadcast_to(upper, (8, ch)), jnp.broadcast_to(lower, (8, ch))], 0
    ).astype(F32)

    def by_cells(array):
        return jnp.transpose(array[0], (1, 2, 0)).reshape(cells, ch)

    part, half = 3 * ch, 3 * ch // 2
    quarter = part // (2 * ny)
    piece = quarter // n_lat
    copies = 2 * ny + 2 * n_lat + n_lon
    vmem = pl.BlockSpec(memory_space=pltpu.VMEM)
    padded = ((rows + 2) * cols, part)
    zeroed = ((rows + 4) * cols, ch)
    out, grad_fields, grad_one, grad_two = pl.pallas_call(
        functools.partial(kernel, (n_lon, n_lat, n_dp, rows, cols, ch)),
        out_shape=[jax.ShapeDtypeStruct((cells, ch), BF16)] * 2
        + [jax.ShapeDtypeStruct((9 * ch, ch), BF16)] * 2,
        in_specs=[vmem] * 5,
        out_specs=[vmem] * 4,
        scratch_shapes=[
            pltpu.VMEM(padded, BF16), pltpu.VMEM(padded, BF16),
            pltpu.VMEM(zeroed, BF16), pltpu.VMEM(zeroed, BF16),
            pltpu.VMEM((ch, cells), BF16), pltpu.VMEM((ch, cells), BF16),
            pltpu.VMEM((cells, ch), F32), pltpu.VMEM((cells, ch), F32), pltpu.VMEM((cells, ch), BF16),
            pltpu.VMEM((4, 8, rows, ch), F32), pltpu.VMEM((4, 8, rows, ch), F32),
            pltpu.VMEM((4, 2, cols, ch), BF16), pltpu.VMEM((4, 2, cols, ch), BF16),
            pltpu.VMEM((6, part, ch), BF16), pltpu.VMEM((6, part, ch), F32), pltpu.VMEM((6, half, ch), BF16),
            pltpu.VMEM((6, half, ch), BF16), pltpu.VMEM((6, half, ch), F32), pltpu.VMEM((6, ny - 1, quarter, ch), BF16),
            pltpu.VMEM((6, quarter, ch), BF16), pltpu.VMEM((6, quarter, ch), F32), pltpu.VMEM((6, n_lat - 1, piece, ch), BF16),
            pltpu.VMEM((6, n_lon, piece, ch), BF16),
            pltpu.SemaphoreType.DMA((4, 8)), pltpu.SemaphoreType.DMA((4, 8)),
            pltpu.SemaphoreType.DMA((6, copies)), pltpu.SemaphoreType.DMA((6, copies)),
        ],
        compiler_params=pltpu.CompilerParams(
            collective_id=0, has_side_effects=True, vmem_limit_bytes=52 * 1024 * 1024
        ),
        cost_estimate=pl.CostEstimate(
            flops=12 * 9 * ch * ch * cells, bytes_accessed=8 * 9 * ch * ch, transcendentals=2 * cells * ch
        ),
    )(by_cells(fields), by_cells(cotangent), weight_one, weight_two, flips)

    def by_channels(array):
        return jnp.transpose(array.reshape(rows, cols, ch), (2, 0, 1))[None]

    return (
        by_channels(out),
        by_channels(grad_fields),
        grad_one.reshape(9, ch, ch).astype(F32),
        grad_two.reshape(9, ch, ch).astype(F32),
    )


def solution(mesh):
    tile = P("dp", None, "lat", "lon")
    sizes = tuple(mesh.shape[axis] for axis in ("lon", "lat", "dp"))
    return jax.shard_map(
        functools.partial(per_device, sizes), mesh=mesh,
        in_specs=(tile, P(), P(), P(), tile), out_specs=(tile, tile, P(), P()), check_vma=False,
    )
```

time: 319 us -> 79.3 us (0.25)
  waiting for transfers between devices: 132 us -> 0 us
  local copies, waits for them, and re-layouts: 82.7 us -> 6.55 us
  Pallas kernels: 0 us -> 67.9 us
  matrix products: 46.7 us -> 0 us
  starting transfers between devices: 30.9 us -> 0 us
  between operations: 14.8 us -> 0.7 us
  other arithmetic: 10.4 us -> 3.91 us
    psum x1 -> x0, waiting for transfers between devices: 118 us -> none  [per_device(): grad_one, grad_two = lax.psum((local_one, local_two), ('lon', 'lat', 'dp'))]
    pallas_call x0 -> x1, Pallas kernels: none -> 67.9 us  [per_device(): pl.pallas_call(functools.partial(kernel, (n_lon, n_lat, n_dp, rows, cols,...]
    scatter-add x18 -> x0, local copies, waits for them, and re-layouts: 60.1 us -> none  [the longest x14 57 us: transposed(): padded_grad = padded_grad.at[:, :, tap_row:tap_row + tile_rows, tap_col:t...]
    dot_general x22 -> x0, matrix products: 46.7 us -> none  [the longest x18 32.6 us: transposed(): jnp.einsum('oc,bohw->bchw', weight[3 * tap_row + tap_col], grad_tile, pre...]
    ppermute x16 -> x0, starting transfers between devices: 30.9 us -> none  [the longest x8 18.9 us: with_halo(): lax.ppermute(head, axis, [((i + 1) % count, i) for i in range(ends)])]
    unnamed x42 -> x8, local copies, waits for them, and re-layouts: 16.2 us -> 0.65 us
    ppermute x16 -> x0, waiting for transfers between devices: 14.4 us -> none  [the longest x8 8.72 us: with_halo(): lax.ppermute(tail, axis, [(i, (i + 1) % count) for i in range(ends)])]
    convert_element_type x1 -> x3, other arithmetic: 0.12 us -> 3.91 us  [the longest x1 1.63 us: per_device(): grad_one.reshape(9, ch, ch).astype(F32)]
  transfers between devices with their start and end apart: 17 -> 0, of which waited for: 6 -> 0; matrix products, arithmetic and copies ran while one was open for 34% -> 0% of each run, Pallas kernels for 0% -> 0%
where the time goes in v1:
time: 79.3 us; the launch traced here: 79.1 us
  Pallas kernels  67.9 us (86%)
  local copies, waits for them, and re-layouts  6.55 us (8%)
  other arithmetic  3.91 us (5%)
    pallas_call x1, Pallas kernels, per_device(): pl.pallas_call(functools.partial(kernel, (n_lon, n_lat, n_dp, rows, cols,...  67.9 us
    transpose x2, local copies, waits for them, and re-layouts, by_cells(): return jnp.transpose(array[0], (1, 2, 0)).reshape(cells, ch)  2.45 us
    reshape x2, local copies, waits for them, and re-layouts, by_channels(): return jnp.transpose(array.reshape(rows, cols, ch), (2, 0, 1))[None]  2.15 us
    convert_element_type x1, other arithmetic, per_device(): grad_one.reshape(9, ch, ch).astype(F32)  1.63 us
    convert_element_type x1, other arithmetic, per_device(): grad_two.reshape(9, ch, ch).astype(F32)  1.63 us

profile of v1, /device:TPU:0, one launch (start us, length us, event | category | flops | bytes accessed | tf_op | source)
XLA Modules:
  0.0 79.1 jit_solution(4103693803835840596)
XLA Ops:
  0.6 0.0 copy-start
  0.6 0.0 copy-start.3
  0.7 0.6 copy-done
  1.3 0.6 constant_dynamic-slice_fusion
  1.9 0.6 broadcast_in_dim.17
  2.5 0.7 pad_convert_fusion
  3.2 0.1 concatenate.6.flip_ref
  3.3 1.3 %copy.9 = bf16[8,128,256]{2,1,0:T(8,128)(2,1)S(1)} copy(bf16[8,128,256]{1,0,2:T(8,128)(2,1)} %bitcast.26) | data formatting | bytes 1048576 | tf_op jit(solution)/shard_map/transpose | solution.py:373
  4.6 0.0 copy-done.3
  4.6 1.1 %copy.10 = bf16[8,128,256]{2,1,0:T(8,128)(2,1)} copy(bf16[8,128,256]{1,0,2:T(8,128)(2,1)S(1)} %bitcast.27) | data formatting | bytes 1048576 | tf_op jit(solution)/shard_map/transpose | solution.py:373
  5.7 67.9 %shard_map.84 = (bf16[1024,256]{1,0:T(8,128)(2,1)S(1)}, bf16[1024,256]{1,0:T(8,128)(2,1)S(1)}, bf16[2304,256]{1,0:T(8,128)(2,1)}, bf16[2304,256]{1,0:T(8,128)(2,1)}) custom-call(bf16[1024,256]{1,0:T(8,128)(2,1)S(1)} %bitcast.23, bf16[1024,256]{1,0:T(8,128)(2,1)} %bitcast.30, bf16[9,256,256]{2,1,0:T(8,128)(2,1)} %w1_ref.1, bf16[9,256,256]{2,1,0:T(8,128)(2,1)} %w2_ref.1, ...), custom_call_target="tpu_custom_call" | custom-call | flops 7247757312 | bytes 4718592 | tf_op jit(solution)/shard_map/pallas_call | solution.py:382
  73.7 0.0 copy-start.2
  73.7 1.1 %copy.11 = bf16[8,128,256]{1,0,2:T(8,128)(2,1)} copy(bf16[8,128,256]{2,1,0:T(8,128)(2,1)S(1)} %bitcast.22) | data formatting | bytes 1048576 | tf_op jit(solution)/shard_map/reshape | solution.py:411
  74.8 1.1 %copy.12 = bf16[8,128,256]{1,0,2:T(8,128)(2,1)} copy(bf16[8,128,256]{2,1,0:T(8,128)(2,1)S(1)} %bitcast.21) | data formatting | bytes 1048576 | tf_op jit(solution)/shard_map/reshape | solution.py:411
  75.8 0.0 copy-done.2
  75.8 0.0 copy-start.1
  75.8 1.6 %convert.2 = f32[9,256,256]{2,1,0:T(8,128)} convert(bf16[9,256,256]{2,1,0:T(8,128)(2,1)S(1)} %bitcast.25) | non-fusion elementwise | flops 589824 | bytes 3538944 | tf_op jit(solution)/shard_map/convert_element_type | solution.py:416
  77.5 0.0 copy-done.1
  77.5 1.6 %convert.3 = f32[9,256,256]{2,1,0:T(8,128)} convert(bf16[9,256,256]{2,1,0:T(8,128)(2,1)S(1)} %bitcast.24) | non-fusion elementwise | flops 589824 | bytes 3538944 | tf_op jit(solution)/shard_map/convert_element_type | solution.py:417
Async XLA Ops:
  0.6 0.7 copy-start
  0.6 3.9 %copy-start.3 = (bf16[1,256,8,128]{3,2,1,0:T(8,128)(2,1)S(1)}, bf16[1,256,8,128]{3,2,1,0:T(8,128)(2,1)}, u32[]{:S(2)}) copy-start(bf16[1,256,8,128]{3,2,1,0:T(8,128)(2,1)} %param.9) | copy-start | bytes 1572868
  73.7 2.2 %copy-start.2 = (bf16[2304,256]{1,0:T(8,128)(2,1)S(1)}, bf16[2304,256]{1,0:T(8,128)(2,1)}, u32[]{:S(2)}) copy-start(bf16[2304,256]{1,0:T(8,128)(2,1)} %get-tuple-element.10) | copy-start | bytes 3538948
  75.8 1.6 %copy-start.1 = (bf16[2304,256]{1,0:T(8,128)(2,1)S(1)}, bf16[2304,256]{1,0:T(8,128)(2,1)}, u32[]{:S(2)}) copy-start(bf16[2304,256]{1,0:T(8,128)(2,1)} %get-tuple-element.11) | copy-start | bytes 3538948

commit v2 on v1

--- a/solution.py
+++ b/solution.py
@@ -24,7 +24,7 @@
     out_ref, gf_ref, o1_ref, o2_ref,
     x1, x2, gz, bz, gt, bt, q, hid, act,
     cell_out, cell_in, row_out, row_in,
-    s0, a0, r0, s1, a1, r1, s2, a2, r2, near,
+    a0, r0, s1, a1, r1, s2, a2, r2, a3, r3, near, full,
     halo_send, halo_recv, sum_send, sum_recv,
 ):
     n_lon, n_lat, n_dp, rows, cols, ch = sizes
@@ -100,7 +100,9 @@
     ja = lax.broadcasted_iota(jnp.int32, (cols, cols), 0)
     jb = lax.broadcasted_iota(jnp.int32, (cols, cols), 1)
     exchange = jnp.where(ja + jb == cols - 1, 1.0, 0.0).astype(BF16)
-    flip_up, flip_down = flip_ref[0:1, :] > 0.5, flip_ref[8:9, :] > 0.5
+    zero = jnp.zeros((1, ch), jnp.int32)
+    flip_up = zero + flip_ref[jnp.maximum(lat - 1, 0), lon] == 1
+    flip_down = zero + flip_ref[jnp.minimum(lat, n_lat - 2), lon] == 1
 
     def turned(flag, west_cell, middle, east_cell):
         back = product(exchange, middle, NN)
@@ -185,6 +187,7 @@
                     row_out[e, slot] = middle.astype(BF16)
                     cell_out[e, 4 + 2 * slot, 0:1, :] = first
                     cell_out[e, 5 + 2 * slot, 0:1, :] = last
+            tick()
         halo_start(e)
 
     def returned_row(e, h):
@@ -200,114 +203,141 @@
             east_cell = east_cell + cell_in[e, 7, 0:1, :]
         return value + jnp.where(line == 0, west_cell, 0.0) + jnp.where(line == cols - 1, east_cell, 0.0)
 
-    part_rows = 3 * ch
-    half, quarter = part_rows // 2, part_rows // (2 * ny)
-    piece = quarter // n_lat
-
-    def start_all(copies):
-        for copy in copies:
-            copy.start()
-
-    def finish(copies):
-        for copy in copies:
-            copy.wait()
-
-    def gathered(p):
-        ref = o1_ref if p < 3 else o2_ref
-        return lambda start, size: ref.at[pl.ds(pl.multiple_of((p % 3) * part_rows + start, 16), size), :]
-
-    core_at, y_at, lat_at = core * half, core * half + y * quarter, core * half + y * quarter + lat * piece
-    slots = iter(range(1000))
-    sem_core, sem_y, sem_lat, sem_lon, sem_lat2, sem_y2, sem_core2 = (
-        [next(slots) for _ in range(n)] for n in (1, ny - 1, n_lat - 1, n_lon - 1, n_lat - 1, ny - 1, 1)
-    )
-
-    def to_core(p, src, dst, sem):
-        return remote(src, dst, sum_send.at[p, sem], sum_recv.at[p, sem], lon, lat, y * 2 + 1 - core)
-
-    def to_y(p, src, dst, sem, k):
-        return remote(src, dst, sum_send.at[p, sem], sum_recv.at[p, sem], lon, lat, lax.rem(y + k, ny) * 2 + core)
-
-    def to_lat(p, src, dst, sem, k):
-        return remote(src, dst, sum_send.at[p, sem], sum_recv.at[p, sem], lon, lax.rem(lat + k, n_lat), dp)
-
-    def to_lon(p, src, dst, sem, k):
-        return remote(src, dst, sum_send.at[p, sem], sum_recv.at[p, sem], lax.rem(lon + k, n_lon), lat, dp)
+    lanes = ch // 2
+    part_rows = 6 * ch
+    half = part_rows // 2
+    piece = half // (ny * n_lat)
+    strip = piece // n_lon
+    scattered = strip % 16 == 0
 
     def rows_of(start, size):
         return pl.ds(pl.multiple_of(start, 16), size)
 
     def reduce_steps(p, grad):
-        for s in range(3):
-            a0[p, s * ch : (s + 1) * ch, :] = grad[:, s * ch : (s + 1) * ch]
-            s0[p, s * ch : (s + 1) * ch, :] = grad[:, s * ch : (s + 1) * ch].astype(BF16)
-        copies = [to_core(p, s0.at[p, rows_of((1 - core) * half, half), :], r0.at[p], sem_core[0])]
-        start_all(copies)
-        yield
-        finish(copies)
-        total = a0[p, rows_of(core_at, half), :] + r0[p].astype(F32)
+        target = full.at[p]
+        sem = iter(range(1000))
+
+        def send(src, dst, axis, k=1):
+            slot = next(sem)
+            to = {"lon": lon, "lat": lat, "dp": dp}
+            if axis == "core":
+                to["dp"] = y * 2 + 1 - core
+            elif axis == "y":
+                to["dp"] = lax.rem(y + k, ny) * 2 + core
+            elif axis == "lat":
+                to["lat"] = lax.rem(lat + k, n_lat)
+            else:
+                to["lon"] = lax.rem(lon + k, n_lon)
+            copy = remote(
+                src, dst, sum_send.at[p, slot], sum_recv.at[p, slot], to["lon"], to["lat"], to["dp"]
+            )
+            copy.start()
+            return copy
+
+        def finish(copies):
+            for copy in copies:
+                copy.wait()
+
+        first, second = (("y", ny, y), ("lat", n_lat, lat))[:: 1 if p % 2 == 0 else -1]
+        size1 = half // first[1]
+
+        for n in range(6):
+            a0[p, n * ch : (n + 1) * ch, :] = grad[:, n * lanes : (n + 1) * lanes]
+        copies = [send(a0.at[p, rows_of((1 - core) * half, half), :], r0.at[p], "core")]
+        yield
+        finish(copies)
+        total = a0[p, rows_of(core * half, half), :] + r0[p]
         a1[p] = total
         s1[p] = total.astype(BF16)
+        axis, count, mine = first
         copies = [
-            to_y(p, s1.at[p, rows_of(lax.rem(y + k, ny) * quarter, quarter), :], r1.at[p, k - 1], sem_y[k - 1], k)
-            for k in range(1, ny)
+            send(
+                s1.at[p, rows_of(lax.rem(mine + k, count) * size1, size1), :],
+                r1.at[p, (k - 1) * size1 : k * size1, :], axis, k,
+            )
+            for k in range(1, count)
         ]
-        start_all(copies)
-        yield
-        finish(copies)
-        total = a1[p, rows_of(y * quarter, quarter), :]
-        for k in range(1, ny):
-            total = total + r1[p, k - 1].astype(F32)
-        a2[p] = total
-        s2[p] = total.astype(BF16)
+        yield
+        finish(copies)
+        total = a1[p, rows_of(mine * size1, size1), :]
+        for k in range(1, count):
+            total = total + r1[p, (k - 1) * size1 : k * size1, :].astype(F32)
+        a2[p, 0:size1, :] = total
+        s2[p, 0:size1, :] = total.astype(BF16)
+        axis, count, mine = second
         copies = [
-            to_lat(p, s2.at[p, rows_of(lax.rem(lat + k, n_lat) * piece, piece), :], r2.at[p, k - 1], sem_lat[k - 1], k)
-            for k in range(1, n_lat)
+            send(
+                s2.at[p, rows_of(lax.rem(mine + k, count) * piece, piece), :],
+                r2.at[p, (k - 1) * piece : k * piece, :], axis, k,
+            )
+            for k in range(1, count)
         ]
-        start_all(copies)
-        yield
-        finish(copies)
-        total = a2[p, rows_of(lat * piece, piece), :]
-        for k in range(1, n_lat):
-            total = total + r2[p, k - 1].astype(F32)
-        near[p, lon] = total.astype(BF16)
-        copies = [to_lon(p, near.at[p, lon], near.at[p, lon], sem_lon[k - 1], k) for k in range(1, n_lon)]
-        start_all(copies)
-        yield
-        finish(copies)
-        total = near[p, 0].astype(F32)
-        for k in range(1, n_lon):
-            total = total + near[p, k].astype(F32)
-        place = gathered(p)
-        mine = place(lat_at, piece)
-        mine[...] = total.astype(BF16)
-        copies = [to_lat(p, mine, mine, sem_lat2[k - 1], k) for k in range(1, n_lat)]
-        start_all(copies)
-        yield
-        finish(copies)
-        mine = place(y_at, quarter)
-        copies = [to_y(p, mine, mine, sem_y2[k - 1], k) for k in range(1, ny)]
-        start_all(copies)
-        yield
-        finish(copies)
-        mine = place(core_at, half)
-        copies = [to_core(p, mine, mine, sem_core2[0])]
-        start_all(copies)
-        yield
-        finish(copies)
-
+        yield
+        finish(copies)
+        total = a2[p, rows_of(mine * piece, piece), :]
+        for k in range(1, count):
+            total = total + r2[p, (k - 1) * piece : k * piece, :].astype(F32)
+        at1 = core * half + first[2] * size1
+        at2 = at1 + second[2] * piece
+        if scattered:
+            a3[p] = total
+            copies = []
+            for k in range(1, n_lon):
+                there = rows_of(lax.rem(lon + k, n_lon) * strip, strip)
+                copies.append(send(a3.at[p, there, :], r3.at[p, k - 1], "lon", k))
+            yield
+            finish(copies)
+            total = a3[p, rows_of(lon * strip, strip), :]
+            for k in range(1, n_lon):
+                total = total + r3[p, k - 1]
+            own = target.at[rows_of(at2 + lon * strip, strip), :]
+            own[...] = total.astype(BF16)
+            copies = [send(own, own, "lon", k) for k in range(1, n_lon)]
+            yield
+            finish(copies)
+        else:
+            near[p, lon] = total.astype(BF16)
+            copies = [send(near.at[p, lon], near.at[p, lon], "lon", k) for k in range(1, n_lon)]
+            yield
+            finish(copies)
+            total = near[p, 0].astype(F32)
+            for k in range(1, n_lon):
+                total = total + near[p, k].astype(F32)
+            target[rows_of(at2, piece), :] = total.astype(BF16)
+        own = target.at[rows_of(at2, piece), :]
+        copies = [send(own, own, second[0], k) for k in range(1, second[1])]
+        yield
+        finish(copies)
+        own = target.at[rows_of(at1, size1), :]
+        copies = [send(own, own, first[0], k) for k in range(1, first[1])]
+        yield
+        finish(copies)
+        own = target.at[rows_of(core * half, half), :]
+        copies = [send(own, own, "core")]
+        yield
+        finish(copies)
+        result = o1_ref if p < 3 else o2_ref
+        for n in range(6):
+            result[3 * (p % 3) + n // 2, :, (n % 2) * lanes : (n % 2 + 1) * lanes] = full[
+                p, n * ch : (n + 1) * ch, :
+            ]
+
+    patience = (1, 3, 2, 2, 1, 1, 2, 1)
     running = []
 
     def tick():
-        for steps in list(running):
-            if next(steps, "end") == "end":
-                running.remove(steps)
+        for state in list(running):
+            state["age"] += 1
+            if state["age"] >= patience[state["step"]]:
+                state["age"], state["step"] = 0, state["step"] + 1
+                if next(state["steps"], "end") == "end":
+                    running.remove(state)
 
     def begin(p, grad):
-        tick()
         steps = reduce_steps(p, grad)
         next(steps)
-        running.append(steps)
+        tick()
+        running.append({"steps": steps, "age": 0, "step": 0})
 
     pl.semaphore_wait(barrier, greeted)
     send_field(0, x_ref)
@@ -341,10 +371,10 @@
     for r in range(3):
         begin(r, product(bt[...], x1[r * cols : r * cols + cells, :], NN))
     pad_field(1, act, x2)
+    tick()
     for r in range(3):
         begin(3 + r, product(gt[...], x2[r * cols : r * cols + cells, :], NN))
     back_conv(3, bz, w1_ref)
-    tick()
     for i in range(2):
         at = slice(i * block, (i + 1) * block)
         out_ref[at, :] = (x_ref[at, :].astype(F32) + conv(x2, w2_ref, i)).astype(BF16)
@@ -353,6 +383,7 @@
     for h in range(rows):
         at = slice(h * cols, (h + 1) * cols)
         gf_ref[at, :] = (g_ref[at, :].astype(F32) + returned_row(3, h)).astype(BF16)
+    patience = (1,) * 8
     while running:
         tick()
 
@@ -362,28 +393,21 @@
     _, ch, rows, cols = fields.shape
     cells = rows * cols
     ny = n_dp // 2
-    lat, lon = lax.axis_index("lat"), lax.axis_index("lon")
-    upper = lax.dynamic_slice(edge_flips, (jnp.maximum(lat - 1, 0), lon), (1, 1))
-    lower = lax.dynamic_slice(edge_flips, (jnp.minimum(lat, n_lat - 2), lon), (1, 1))
-    flips = jnp.concatenate(
-        [jnp.broadcast_to(upper, (8, ch)), jnp.broadcast_to(lower, (8, ch))], 0
-    ).astype(F32)
-
     def by_cells(array):
         return jnp.transpose(array[0], (1, 2, 0)).reshape(cells, ch)
 
-    part, half = 3 * ch, 3 * ch // 2
-    quarter = part // (2 * ny)
-    piece = quarter // n_lat
-    copies = 2 * ny + 2 * n_lat + n_lon
+    part, half, lanes = 3 * ch, 3 * ch, ch // 2
+    piece = half // (ny * n_lat)
+    strip = max(8, piece // n_lon)
+    copies = 2 * (ny + n_lat + n_lon)
     vmem = pl.BlockSpec(memory_space=pltpu.VMEM)
     padded = ((rows + 2) * cols, part)
     zeroed = ((rows + 4) * cols, ch)
     out, grad_fields, grad_one, grad_two = pl.pallas_call(
         functools.partial(kernel, (n_lon, n_lat, n_dp, rows, cols, ch)),
         out_shape=[jax.ShapeDtypeStruct((cells, ch), BF16)] * 2
-        + [jax.ShapeDtypeStruct((9 * ch, ch), BF16)] * 2,
-        in_specs=[vmem] * 5,
+        + [jax.ShapeDtypeStruct((9, ch, ch), BF16)] * 2,
+        in_specs=[vmem] * 4 + [pl.BlockSpec(memory_space=pltpu.SMEM)],
         out_specs=[vmem] * 4,
         scratch_shapes=[
             pltpu.VMEM(padded, BF16), pltpu.VMEM(padded, BF16),
@@ -392,10 +416,12 @@
             pltpu.VMEM((cells, ch), F32), pltpu.VMEM((cells, ch), F32), pltpu.VMEM((cells, ch), BF16),
             pltpu.VMEM((4, 8, rows, ch), F32), pltpu.VMEM((4, 8, rows, ch), F32),
             pltpu.VMEM((4, 2, cols, ch), BF16), pltpu.VMEM((4, 2, cols, ch), BF16),
-            pltpu.VMEM((6, part, ch), BF16), pltpu.VMEM((6, part, ch), F32), pltpu.VMEM((6, half, ch), BF16),
-            pltpu.VMEM((6, half, ch), BF16), pltpu.VMEM((6, half, ch), F32), pltpu.VMEM((6, ny - 1, quarter, ch), BF16),
-            pltpu.VMEM((6, quarter, ch), BF16), pltpu.VMEM((6, quarter, ch), F32), pltpu.VMEM((6, n_lat - 1, piece, ch), BF16),
-            pltpu.VMEM((6, n_lon, piece, ch), BF16),
+            pltpu.VMEM((6, 6 * ch, lanes), F32), pltpu.VMEM((6, half, lanes), F32),
+            pltpu.VMEM((6, half, lanes), BF16), pltpu.VMEM((6, half, lanes), F32), pltpu.VMEM((6, half, lanes), BF16),
+            pltpu.VMEM((6, half // 2, lanes), BF16), pltpu.VMEM((6, half // 2, lanes), F32),
+            pltpu.VMEM((6, half // 2, lanes), BF16),
+            pltpu.VMEM((6, piece, lanes), F32), pltpu.VMEM((6, n_lon - 1, strip, lanes), F32),
+            pltpu.VMEM((6, n_lon, piece, lanes), BF16), pltpu.VMEM((6, 6 * ch, lanes), BF16),
             pltpu.SemaphoreType.DMA((4, 8)), pltpu.SemaphoreType.DMA((4, 8)),
             pltpu.SemaphoreType.DMA((6, copies)), pltpu.SemaphoreType.DMA((6, copies)),
         ],
@@ -405,7 +431,7 @@
         cost_estimate=pl.CostEstimate(
             flops=12 * 9 * ch * ch * cells, bytes_accessed=8 * 9 * ch * ch, transcendentals=2 * cells * ch
         ),
-    )(by_cells(fields), by_cells(cotangent), weight_one, weight_two, flips)
+    )(by_cells(fields), by_cells(cotangent), weight_one, weight_two, edge_flips)
 
     def by_channels(array):
         return jnp.transpose(array.reshape(rows, cols, ch), (2, 0, 1))[None]
@@ -413,8 +439,8 @@
     return (
         by_channels(out),
         by_channels(grad_fields),
-        grad_one.reshape(9, ch, ch).astype(F32),
-        grad_two.reshape(9, ch, ch).astype(F32),
+        grad_one.astype(F32),
+        grad_two.astype(F32),
     )
 
 

time: 79.3 us -> 72.5 us (0.914)
  Pallas kernels: 67.9 us -> 63.7 us
  local copies, waits for them, and re-layouts: 6.55 us -> 4.67 us
    pallas_call x1, Pallas kernels: 67.9 us -> 63.7 us  [per_device(): pl.pallas_call(functools.partial(kernel, (n_lon, n_lat, n_dp, rows, cols,...]
    convert_element_type x3 -> x2, other arithmetic: 3.91 us -> 3.26 us  [the longest x1 1.63 us: per_device(): grad_one.astype(F32)]
where the time goes in v2:
time: 72.5 us; the launch traced here: 72.3 us
  Pallas kernels  63.7 us (88%)
  local copies, waits for them, and re-layouts  4.67 us (6%)
  other arithmetic  3.26 us (4%)
    pallas_call x1, Pallas kernels, per_device(): pl.pallas_call(functools.partial(kernel, (n_lon, n_lat, n_dp, rows, cols,...  63.7 us
    transpose x2, local copies, waits for them, and re-layouts, by_cells(): return jnp.transpose(array[0], (1, 2, 0)).reshape(cells, ch)  2.5 us
    reshape x2, local copies, waits for them, and re-layouts, by_channels(): return jnp.transpose(array.reshape(rows, cols, ch), (2, 0, 1))[None]  2.15 us
    convert_element_type x1, other arithmetic, per_device(): grad_one.astype(F32)  1.63 us
    convert_element_type x1, other arithmetic, per_device(): grad_two.astype(F32)  1.63 us

profile of v2, /device:TPU:0, one launch (start us, length us, event | category | flops | bytes accessed | tf_op | source)
XLA Modules:
  0.0 72.3 jit_solution(8064790848482093560)
XLA Ops:
  0.6 0.0 copy-start.3
  0.6 0.0 copy-start
  0.7 1.4 %copy.9 = bf16[8,128,256]{2,1,0:T(8,128)(2,1)S(1)} copy(bf16[8,128,256]{1,0,2:T(8,128)(2,1)} %bitcast.19) | data formatting | bytes 1048576 | tf_op jit(solution)/shard_map/transpose | solution.py:397
  2.0 0.0 copy-done.3
  2.0 1.1 %copy.10 = bf16[8,128,256]{2,1,0:T(8,128)(2,1)} copy(bf16[8,128,256]{1,0,2:T(8,128)(2,1)S(1)} %bitcast.20) | data formatting | bytes 1048576 | tf_op jit(solution)/shard_map/transpose | solution.py:397
  3.2 0.0 copy-done
  3.2 63.7 %shard_map.84 = (bf16[1024,256]{1,0:T(8,128)(2,1)S(1)}, bf16[1024,256]{1,0:T(8,128)(2,1)S(1)}, bf16[9,256,256]{2,1,0:T(8,128)(2,1)}, bf16[9,256,256]{2,1,0:T(8,128)(2,1)}) custom-call(bf16[1024,256]{1,0:T(8,128)(2,1)S(1)} %bitcast.18, bf16[1024,256]{1,0:T(8,128)(2,1)} %bitcast.23, bf16[9,256,256]{2,1,0:T(8,128)(2,1)} %w1_ref.1, bf16[9,256,256]{2,1,0:T(8,128)(2,1)} %w2_ref.1, ...), custom_call_target="tpu_custom_call" | custom-call | flops 7247757312 | bytes 4718592 | tf_op jit(solution)/shard_map/pallas_call | solution.py:406
  66.9 0.0 copy-start.2
  66.9 1.1 %copy.11 = bf16[8,128,256]{1,0,2:T(8,128)(2,1)} copy(bf16[8,128,256]{2,1,0:T(8,128)(2,1)S(1)} %bitcast.17) | data formatting | bytes 1048576 | tf_op jit(solution)/shard_map/reshape | solution.py:437
  68.0 1.1 %copy.12 = bf16[8,128,256]{1,0,2:T(8,128)(2,1)} copy(bf16[8,128,256]{2,1,0:T(8,128)(2,1)S(1)} %bitcast.16) | data formatting | bytes 1048576 | tf_op jit(solution)/shard_map/reshape | solution.py:437
  69.0 0.0 copy-done.2
  69.0 0.0 copy-start.1
  69.1 1.6 %convert_element_type.6 = f32[9,256,256]{2,1,0:T(8,128)} convert(bf16[9,256,256]{2,1,0:T(8,128)(2,1)S(1)} %copy-done.2) | non-fusion elementwise | flops 589824 | bytes 3538944 | tf_op jit(solution)/shard_map/convert_element_type | solution.py:442
  70.7 0.0 copy-done.1
  70.7 1.6 %convert_element_type.7 = f32[9,256,256]{2,1,0:T(8,128)} convert(bf16[9,256,256]{2,1,0:T(8,128)(2,1)S(1)} %copy-done.1) | non-fusion elementwise | flops 589824 | bytes 3538944 | tf_op jit(solution)/shard_map/convert_element_type | solution.py:443
Async XLA Ops:
  0.6 1.4 %copy-start.3 = (bf16[1,256,8,128]{3,2,1,0:T(8,128)(2,1)S(1)}, bf16[1,256,8,128]{3,2,1,0:T(8,128)(2,1)}, u32[]{:S(2)}) copy-start(bf16[1,256,8,128]{3,2,1,0:T(8,128)(2,1)} %param.9) | copy-start | bytes 1572868
  0.6 2.5 %copy-start = (s32[1,4]{1,0:T(1,128)S(1)}, s32[1,4]{1,0:T(1,128)}, u32[]{:S(2)}) copy-start(s32[1,4]{1,0:T(1,128)} %flip_ref.1) | copy-start | bytes 52
  66.9 2.2 %copy-start.2 = (bf16[9,256,256]{2,1,0:T(8,128)(2,1)S(1)}, bf16[9,256,256]{2,1,0:T(8,128)(2,1)}, u32[]{:S(2)}) copy-start(bf16[9,256,256]{2,1,0:T(8,128)(2,1)} %get-tuple-element.10) | copy-start | bytes 3538948
  69.0 1.6 %copy-start.1 = (bf16[9,256,256]{2,1,0:T(8,128)(2,1)S(1)}, bf16[9,256,256]{2,1,0:T(8,128)(2,1)}, u32[]{:S(2)}) copy-start(bf16[9,256,256]{2,1,0:T(8,128)(2,1)} %get-tuple-element.11) | copy-start | bytes 3538948

commit v3 on v2

--- a/solution.py
+++ b/solution.py
@@ -24,7 +24,7 @@
     out_ref, gf_ref, o1_ref, o2_ref,
     x1, x2, gz, bz, gt, bt, q, hid, act,
     cell_out, cell_in, row_out, row_in,
-    a0, r0, s1, a1, r1, s2, a2, r2, a3, r3, near, full,
+    a0, r0, s1, a1, r1, a3, r3, near, full,
     halo_send, halo_recv, sum_send, sum_recv,
 ):
     n_lon, n_lat, n_dp, rows, cols, ch = sizes
@@ -57,6 +57,17 @@
             device_id_type=pl.DeviceIdType.MESH,
         )
         greeted += 1
+
+    for k in range(1, ny):
+        for j in range(1, n_lat):
+            pl.semaphore_signal(
+                barrier, inc=1,
+                device_id={
+                    "lon": lon, "lat": lax.rem(lat + j, n_lat), "dp": lax.rem(y + k, ny) * 2 + core,
+                },
+                device_id_type=pl.DeviceIdType.MESH,
+            )
+            greeted += 1
 
     def remote(src, dst, send, recv, to_lon, to_lat, to_dp):
         return pltpu.make_async_remote_copy(
@@ -213,6 +224,11 @@
     def rows_of(start, size):
         return pl.ds(pl.multiple_of(start, 16), size)
 
+    plane = ny * n_lat
+
+    def plane_place(k):
+        return lax.rem(y + k // n_lat, ny) * n_lat + lax.rem(lat + k % n_lat, n_lat)
+
     def reduce_steps(p, grad):
         target = full.at[p]
         sem = iter(range(1000))
@@ -222,10 +238,9 @@
             to = {"lon": lon, "lat": lat, "dp": dp}
             if axis == "core":
                 to["dp"] = y * 2 + 1 - core
-            elif axis == "y":
-                to["dp"] = lax.rem(y + k, ny) * 2 + core
-            elif axis == "lat":
-                to["lat"] = lax.rem(lat + k, n_lat)
+            elif axis == "plane":
+                to["dp"] = lax.rem(y + k // n_lat, ny) * 2 + core
+                to["lat"] = lax.rem(lat + k % n_lat, n_lat)
             else:
                 to["lon"] = lax.rem(lon + k, n_lon)
             copy = remote(
@@ -237,9 +252,6 @@
         def finish(copies):
             for copy in copies:
                 copy.wait()
-
-        first, second = (("y", ny, y), ("lat", n_lat, lat))[:: 1 if p % 2 == 0 else -1]
-        size1 = half // first[1]
 
         for n in range(6):
             a0[p, n * ch : (n + 1) * ch, :] = grad[:, n * lanes : (n + 1) * lanes]
@@ -249,36 +261,16 @@
         total = a0[p, rows_of(core * half, half), :] + r0[p]
         a1[p] = total
         s1[p] = total.astype(BF16)
-        axis, count, mine = first
-        copies = [
-            send(
-                s1.at[p, rows_of(lax.rem(mine + k, count) * size1, size1), :],
-                r1.at[p, (k - 1) * size1 : k * size1, :], axis, k,
-            )
-            for k in range(1, count)
-        ]
+        copies = []
+        for k in range(1, plane):
+            there = rows_of(plane_place(k) * piece, piece)
+            copies.append(send(s1.at[p, there, :], r1.at[p, (k - 1) * piece : k * piece, :], "plane", k))
         yield
         finish(copies)
-        total = a1[p, rows_of(mine * size1, size1), :]
-        for k in range(1, count):
-            total = total + r1[p, (k - 1) * size1 : k * size1, :].astype(F32)
-        a2[p, 0:size1, :] = total
-        s2[p, 0:size1, :] = total.astype(BF16)
-        axis, count, mine = second
-        copies = [
-            send(
-                s2.at[p, rows_of(lax.rem(mine + k, count) * piece, piece), :],
-                r2.at[p, (k - 1) * piece : k * piece, :], axis, k,
-            )
-            for k in range(1, count)
-        ]
-        yield
-        finish(copies)
-        total = a2[p, rows_of(mine * piece, piece), :]
-        for k in range(1, count):
-            total = total + r2[p, (k - 1) * piece : k * piece, :].astype(F32)
-        at1 = core * half + first[2] * size1
-        at2 = at1 + second[2] * piece
+        total = a1[p, rows_of(plane_place(0) * piece, piece), :]
+        for k in range(1, plane):
+            total = total + r1[p, (k - 1) * piece : k * piece, :].astype(F32)
+        at2 = core * half + plane_place(0) * piece
         if scattered:
             a3[p] = total
             copies = []
@@ -305,11 +297,7 @@
                 total = total + near[p, k].astype(F32)
             target[rows_of(at2, piece), :] = total.astype(BF16)
         own = target.at[rows_of(at2, piece), :]
-        copies = [send(own, own, second[0], k) for k in range(1, second[1])]
-        yield
-        finish(copies)
-        own = target.at[rows_of(at1, size1), :]
-        copies = [send(own, own, first[0], k) for k in range(1, first[1])]
+        copies = [send(own, own, "plane", k) for k in range(1, plane)]
         yield
         finish(copies)
         own = target.at[rows_of(core * half, half), :]
@@ -322,7 +310,7 @@
                 p, n * ch : (n + 1) * ch, :
             ]
 
-    patience = (1, 3, 2, 2, 1, 1, 2, 1)
+    patience = (2, 3, 2, 2, 3, 1)
     running = []
 
     def tick():
@@ -338,9 +326,6 @@
         next(steps)
         tick()
         running.append({"steps": steps, "age": 0, "step": 0})
-
-    pl.semaphore_wait(barrier, greeted)
-    send_field(0, x_ref)
 
     edge = jnp.zeros((2 * cols, ch), BF16)
     for z in (gz, bz):
@@ -350,6 +335,8 @@
         value = g_ref[h * cols : (h + 1) * cols, :]
         gz[(h + 2) * cols : (h + 3) * cols, :] = value
         gt[:, h * cols : (h + 1) * cols] = value.astype(F32).T.astype(BF16)
+    pl.semaphore_wait(barrier, greeted)
+    send_field(0, x_ref)
     back_conv(2, gz, w2_ref)
 
     pad_field(0, x_ref, x1)
@@ -399,7 +386,7 @@
     part, half, lanes = 3 * ch, 3 * ch, ch // 2
     piece = half // (ny * n_lat)
     strip = max(8, piece // n_lon)
-    copies = 2 * (ny + n_lat + n_lon)
+    copies = 2 * (ny * n_lat + n_lon)
     vmem = pl.BlockSpec(memory_space=pltpu.VMEM)
     padded = ((rows + 2) * cols, part)
     zeroed = ((rows + 4) * cols, ch)
@@ -418,8 +405,6 @@
             pltpu.VMEM((4, 2, cols, ch), BF16), pltpu.VMEM((4, 2, cols, ch), BF16),
             pltpu.VMEM((6, 6 * ch, lanes), F32), pltpu.VMEM((6, half, lanes), F32),
             pltpu.VMEM((6, half, lanes), BF16), pltpu.VMEM((6, half, lanes), F32), pltpu.VMEM((6, half, lanes), BF16),
-            pltpu.VMEM((6, half // 2, lanes), BF16), pltpu.VMEM((6, half // 2, lanes), F32),
-            pltpu.VMEM((6, half // 2, lanes), BF16),
             pltpu.VMEM((6, piece, lanes), F32), pltpu.VMEM((6, n_lon - 1, strip, lanes), F32),
             pltpu.VMEM((6, n_lon, piece, lanes), BF16), pltpu.VMEM((6, 6 * ch, lanes), BF16),
             pltpu.SemaphoreType.DMA((4, 8)), pltpu.SemaphoreType.DMA((4, 8)),

time: 72.5 us -> 66.1 us (0.912)
  Pallas kernels: 63.7 us -> 57.3 us
    pallas_call x1, Pallas kernels: 63.7 us -> 57.3 us  [per_device(): pl.pallas_call(functools.partial(kernel, (n_lon, n_lat, n_dp, rows, cols,...]
where the time goes in v3:
time: 66.1 us; the launch traced here: 65.9 us
  Pallas kernels  57.3 us (87%)
  local copies, waits for them, and re-layouts  4.67 us (7%)
  other arithmetic  3.26 us (5%)
  between operations  0.68 us (1%)
    pallas_call x1, Pallas kernels, per_device(): pl.pallas_call(functools.partial(kernel, (n_lon, n_lat, n_dp, rows, cols,...  57.3 us
    transpose x2, local copies, waits for them, and re-layouts, by_cells(): return jnp.transpose(array[0], (1, 2, 0)).reshape(cells, ch)  2.5 us
    reshape x2, local copies, waits for them, and re-layouts, by_channels(): return jnp.transpose(array.reshape(rows, cols, ch), (2, 0, 1))[None]  2.15 us
    convert_element_type x1, other arithmetic, per_device(): grad_one.astype(F32)  1.63 us
    convert_element_type x1, other arithmetic, per_device(): grad_two.astype(F32)  1.63 us

profile of v3, /device:TPU:0, one launch (start us, length us, event | category | flops | bytes accessed | tf_op | source)
XLA Modules:
  0.0 65.9 jit_solution(10244672073562922612)
XLA Ops:
  0.6 0.0 copy-start.3
  0.6 0.0 copy-start
  0.7 1.4 %copy.9 = bf16[8,128,256]{2,1,0:T(8,128)(2,1)S(1)} copy(bf16[8,128,256]{1,0,2:T(8,128)(2,1)} %bitcast.19) | data formatting | bytes 1048576 | tf_op jit(solution)/shard_map/transpose | solution.py:384
  2.0 0.0 copy-done.3
  2.0 1.1 %copy.10 = bf16[8,128,256]{2,1,0:T(8,128)(2,1)} copy(bf16[8,128,256]{1,0,2:T(8,128)(2,1)S(1)} %bitcast.20) | data formatting | bytes 1048576 | tf_op jit(solution)/shard_map/transpose | solution.py:384
  3.2 0.0 copy-done
  3.2 57.3 %shard_map.84 = (bf16[1024,256]{1,0:T(8,128)(2,1)S(1)}, bf16[1024,256]{1,0:T(8,128)(2,1)S(1)}, bf16[9,256,256]{2,1,0:T(8,128)(2,1)}, bf16[9,256,256]{2,1,0:T(8,128)(2,1)}) custom-call(bf16[1024,256]{1,0:T(8,128)(2,1)S(1)} %bitcast.18, bf16[1024,256]{1,0:T(8,128)(2,1)} %bitcast.23, bf16[9,256,256]{2,1,0:T(8,128)(2,1)} %w1_ref.1, bf16[9,256,256]{2,1,0:T(8,128)(2,1)} %w2_ref.1, ...), custom_call_target="tpu_custom_call" | custom-call | flops 7247757312 | bytes 4718592 | tf_op jit(solution)/shard_map/pallas_call | solution.py:393
  60.5 0.0 copy-start.2
  60.5 1.1 %copy.11 = bf16[8,128,256]{1,0,2:T(8,128)(2,1)} copy(bf16[8,128,256]{2,1,0:T(8,128)(2,1)S(1)} %bitcast.17) | data formatting | bytes 1048576 | tf_op jit(solution)/shard_map/reshape | solution.py:422
  61.6 1.1 %copy.12 = bf16[8,128,256]{1,0,2:T(8,128)(2,1)} copy(bf16[8,128,256]{2,1,0:T(8,128)(2,1)S(1)} %bitcast.16) | data formatting | bytes 1048576 | tf_op jit(solution)/shard_map/reshape | solution.py:422
  62.7 0.0 copy-done.2
  62.7 0.0 copy-start.1
  62.7 1.6 %convert_element_type.6 = f32[9,256,256]{2,1,0:T(8,128)} convert(bf16[9,256,256]{2,1,0:T(8,128)(2,1)S(1)} %copy-done.2) | non-fusion elementwise | flops 589824 | bytes 3538944 | tf_op jit(solution)/shard_map/convert_element_type | solution.py:427
  64.3 0.0 copy-done.1
  64.3 1.6 %convert_element_type.7 = f32[9,256,256]{2,1,0:T(8,128)} convert(bf16[9,256,256]{2,1,0:T(8,128)(2,1)S(1)} %copy-done.1) | non-fusion elementwise | flops 589824 | bytes 3538944 | tf_op jit(solution)/shard_map/convert_element_type | solution.py:428
Async XLA Ops:
  0.6 1.4 %copy-start.3 = (bf16[1,256,8,128]{3,2,1,0:T(8,128)(2,1)S(1)}, bf16[1,256,8,128]{3,2,1,0:T(8,128)(2,1)}, u32[]{:S(2)}) copy-start(bf16[1,256,8,128]{3,2,1,0:T(8,128)(2,1)} %param.9) | copy-start | bytes 1572868
  0.6 2.5 %copy-start = (s32[1,4]{1,0:T(1,128)S(1)}, s32[1,4]{1,0:T(1,128)}, u32[]{:S(2)}) copy-start(s32[1,4]{1,0:T(1,128)} %flip_ref.1) | copy-start | bytes 52
  60.5 2.2 %copy-start.2 = (bf16[9,256,256]{2,1,0:T(8,128)(2,1)S(1)}, bf16[9,256,256]{2,1,0:T(8,128)(2,1)}, u32[]{:S(2)}) copy-start(bf16[9,256,256]{2,1,0:T(8,128)(2,1)} %get-tuple-element.10) | copy-start | bytes 3538948
  62.7 1.6 %copy-start.1 = (bf16[9,256,256]{2,1,0:T(8,128)(2,1)S(1)}, bf16[9,256,256]{2,1,0:T(8,128)(2,1)}, u32[]{:S(2)}) copy-start(bf16[9,256,256]{2,1,0:T(8,128)(2,1)} %get-tuple-element.11) | copy-start | bytes 3538948

commit v4 on v3

--- a/solution.py
+++ b/solution.py
@@ -22,7 +22,7 @@
     sizes,
     x_ref, g_ref, w1_ref, w2_ref, flip_ref,
     out_ref, gf_ref, o1_ref, o2_ref,
-    x1, x2, gz, bz, gt, bt, q, hid, act,
+    x1, x2, gz, bz, gt, bt, q, slope, act,
     cell_out, cell_in, row_out, row_in,
     a0, r0, s1, a1, r1, a3, r3, near, full,
     halo_send, halo_recv, sum_send, sum_recv,
@@ -166,7 +166,7 @@
         right = jnp.concatenate([w_ref[t] for t in range(9)], 1)
         return product(left, right, NT)
 
-    def back_conv(e, z, w_ref):
+    def back_conv(e, z, w_ref, after=((), ())):
         step = (rows + 2) // 2
         size = step * cols
         for i in range(2):
@@ -198,7 +198,7 @@
                     row_out[e, slot] = middle.astype(BF16)
                     cell_out[e, 4 + 2 * slot, 0:1, :] = first
                     cell_out[e, 5 + 2 * slot, 0:1, :] = last
-            tick()
+            advance(*after[i])
         halo_start(e)
 
     def returned_row(e, h):
@@ -310,22 +310,16 @@
                 p, n * ch : (n + 1) * ch, :
             ]
 
-    patience = (2, 3, 2, 2, 3, 1)
-    running = []
-
-    def tick():
-        for state in list(running):
-            state["age"] += 1
-            if state["age"] >= patience[state["step"]]:
-                state["age"], state["step"] = 0, state["step"] + 1
-                if next(state["steps"], "end") == "end":
-                    running.remove(state)
+    running = {}
+
+    def advance(*parts):
+        for p in parts:
+            if p in running and next(running[p], "end") == "end":
+                del running[p]
 
     def begin(p, grad):
-        steps = reduce_steps(p, grad)
-        next(steps)
-        tick()
-        running.append({"steps": steps, "age": 0, "step": 0})
+        running[p] = reduce_steps(p, grad)
+        next(running[p])
 
     edge = jnp.zeros((2 * cols, ch), BF16)
     for z in (gz, bz):
@@ -341,38 +335,38 @@
 
     pad_field(0, x_ref, x1)
     for i in range(2):
+        at = slice(i * block, (i + 1) * block)
         value = conv(x1, w1_ref, i)
-        hid[i * block : (i + 1) * block, :] = value
-        act[i * block : (i + 1) * block, :] = (value / (1.0 + jnp.exp(-value))).astype(BF16)
+        sigma = 1.0 / (1.0 + jnp.exp(-value))
+        act[at, :] = (value * sigma).astype(BF16)
+        slope[at, :] = sigma * (1.0 + value * (1.0 - sigma))
     send_field(1, act)
 
     halo_wait(2)
     for h in range(rows):
-        back = returned_row(2, h)
-        value = hid[h * cols : (h + 1) * cols, :]
-        sigma = 1.0 / (1.0 + jnp.exp(-value))
-        back = back * sigma * (1.0 + value * (1.0 - sigma))
+        back = returned_row(2, h) * slope[h * cols : (h + 1) * cols, :]
         bz[(h + 2) * cols : (h + 3) * cols, :] = back.astype(BF16)
         bt[:, h * cols : (h + 1) * cols] = back.T.astype(BF16)
 
-    for r in range(3):
+    for r, ready in enumerate(((), (), (0,))):
         begin(r, product(bt[...], x1[r * cols : r * cols + cells, :], NN))
+        advance(*ready)
     pad_field(1, act, x2)
-    tick()
-    for r in range(3):
+    advance(1)
+    for r, ready in enumerate(((2,), (0,), (3,))):
         begin(3 + r, product(gt[...], x2[r * cols : r * cols + cells, :], NN))
-    back_conv(3, bz, w1_ref)
-    for i in range(2):
+        advance(*ready)
+    back_conv(3, bz, w1_ref, ((4, 5, 1), (0, 2)))
+    for i, ready in enumerate(((1, 3), (0, 2, 4))):
         at = slice(i * block, (i + 1) * block)
         out_ref[at, :] = (x_ref[at, :].astype(F32) + conv(x2, w2_ref, i)).astype(BF16)
-        tick()
+        advance(*ready)
     halo_wait(3)
     for h in range(rows):
         at = slice(h * cols, (h + 1) * cols)
         gf_ref[at, :] = (g_ref[at, :].astype(F32) + returned_row(3, h)).astype(BF16)
-    patience = (1,) * 8
     while running:
-        tick()
+        advance(*sorted(running, reverse=True))
 
 
 def per_device(sizes, fields, weight_one, weight_two, edge_flips, cotangent):

time: 66.1 us -> 63.8 us (0.965)
  Pallas kernels: 57.3 us -> 55 us
    pallas_call x1, Pallas kernels: 57.3 us -> 55 us  [per_device(): pl.pallas_call(functools.partial(kernel, (n_lon, n_lat, n_dp, rows, cols,...]
where the time goes in v4:
time: 63.8 us; the launch traced here: 63.6 us
  Pallas kernels  55 us (86%)
  local copies, waits for them, and re-layouts  4.67 us (7%)
  other arithmetic  3.26 us (5%)
  between operations  0.68 us (1%)
    pallas_call x1, Pallas kernels, per_device(): pl.pallas_call(functools.partial(kernel, (n_lon, n_lat, n_dp, rows, cols,...  55 us
    transpose x2, local copies, waits for them, and re-layouts, by_cells(): return jnp.transpose(array[0], (1, 2, 0)).reshape(cells, ch)  2.5 us
    reshape x2, local copies, waits for them, and re-layouts, by_channels(): return jnp.transpose(array.reshape(rows, cols, ch), (2, 0, 1))[None]  2.15 us
    convert_element_type x1, other arithmetic, per_device(): grad_one.astype(F32)  1.63 us
    convert_element_type x1, other arithmetic, per_device(): grad_two.astype(F32)  1.63 us

profile of v4, /device:TPU:0, one launch (start us, length us, event | category | flops | bytes accessed | tf_op | source)
XLA Modules:
  0.0 63.6 jit_solution(8104861371815823519)
XLA Ops:
  0.6 0.0 copy-start.3
  0.6 0.0 copy-start
  0.7 1.4 %copy.9 = bf16[8,128,256]{2,1,0:T(8,128)(2,1)S(1)} copy(bf16[8,128,256]{1,0,2:T(8,128)(2,1)} %bitcast.19) | data formatting | bytes 1048576 | tf_op jit(solution)/shard_map/transpose | solution.py:378
  2.0 0.0 copy-done.3
  2.0 1.1 %copy.10 = bf16[8,128,256]{2,1,0:T(8,128)(2,1)} copy(bf16[8,128,256]{1,0,2:T(8,128)(2,1)S(1)} %bitcast.20) | data formatting | bytes 1048576 | tf_op jit(solution)/shard_map/transpose | solution.py:378
  3.2 0.0 copy-done
  3.2 55.0 %shard_map.84 = (bf16[1024,256]{1,0:T(8,128)(2,1)S(1)}, bf16[1024,256]{1,0:T(8,128)(2,1)S(1)}, bf16[9,256,256]{2,1,0:T(8,128)(2,1)}, bf16[9,256,256]{2,1,0:T(8,128)(2,1)}) custom-call(bf16[1024,256]{1,0:T(8,128)(2,1)S(1)} %bitcast.18, bf16[1024,256]{1,0:T(8,128)(2,1)} %bitcast.23, bf16[9,256,256]{2,1,0:T(8,128)(2,1)} %w1_ref.1, bf16[9,256,256]{2,1,0:T(8,128)(2,1)} %w2_ref.1, ...), custom_call_target="tpu_custom_call" | custom-call | flops 7247757312 | bytes 4718592 | tf_op jit(solution)/shard_map/pallas_call | solution.py:387
  58.2 0.0 copy-start.2
  58.2 1.1 %copy.11 = bf16[8,128,256]{1,0,2:T(8,128)(2,1)} copy(bf16[8,128,256]{2,1,0:T(8,128)(2,1)S(1)} %bitcast.17) | data formatting | bytes 1048576 | tf_op jit(solution)/shard_map/reshape | solution.py:416
  59.3 1.1 %copy.12 = bf16[8,128,256]{1,0,2:T(8,128)(2,1)} copy(bf16[8,128,256]{2,1,0:T(8,128)(2,1)S(1)} %bitcast.16) | data formatting | bytes 1048576 | tf_op jit(solution)/shard_map/reshape | solution.py:416
  60.3 0.0 copy-done.2
  60.3 0.0 copy-start.1
  60.3 1.6 %convert_element_type.6 = f32[9,256,256]{2,1,0:T(8,128)} convert(bf16[9,256,256]{2,1,0:T(8,128)(2,1)S(1)} %copy-done.2) | non-fusion elementwise | flops 589824 | bytes 3538944 | tf_op jit(solution)/shard_map/convert_element_type | solution.py:421
  62.0 0.0 copy-done.1
  62.0 1.6 %convert_element_type.7 = f32[9,256,256]{2,1,0:T(8,128)} convert(bf16[9,256,256]{2,1,0:T(8,128)(2,1)S(1)} %copy-done.1) | non-fusion elementwise | flops 589824 | bytes 3538944 | tf_op jit(solution)/shard_map/convert_element_type | solution.py:422
Async XLA Ops:
  0.6 1.4 %copy-start.3 = (bf16[1,256,8,128]{3,2,1,0:T(8,128)(2,1)S(1)}, bf16[1,256,8,128]{3,2,1,0:T(8,128)(2,1)}, u32[]{:S(2)}) copy-start(bf16[1,256,8,128]{3,2,1,0:T(8,128)(2,1)} %param.9) | copy-start | bytes 1572868
  0.6 2.5 %copy-start = (s32[1,4]{1,0:T(1,128)S(1)}, s32[1,4]{1,0:T(1,128)}, u32[]{:S(2)}) copy-start(s32[1,4]{1,0:T(1,128)} %flip_ref.1) | copy-start | bytes 52
  58.2 2.2 %copy-start.2 = (bf16[9,256,256]{2,1,0:T(8,128)(2,1)S(1)}, bf16[9,256,256]{2,1,0:T(8,128)(2,1)}, u32[]{:S(2)}) copy-start(bf16[9,256,256]{2,1,0:T(8,128)(2,1)} %get-tuple-element.10) | copy-start | bytes 3538948
  60.3 1.6 %copy-start.1 = (bf16[9,256,256]{2,1,0:T(8,128)(2,1)S(1)}, bf16[9,256,256]{2,1,0:T(8,128)(2,1)}, u32[]{:S(2)}) copy-start(bf16[9,256,256]{2,1,0:T(8,128)(2,1)} %get-tuple-element.11) | copy-start | bytes 3538948

commit v5 on v4

--- a/solution.py
+++ b/solution.py
@@ -24,7 +24,7 @@
     out_ref, gf_ref, o1_ref, o2_ref,
     x1, x2, gz, bz, gt, bt, q, slope, act,
     cell_out, cell_in, row_out, row_in,
-    a0, r0, s1, a1, r1, a3, r3, near, full,
+    a0, r0, s1, a1, r1, s2, a2, r2, a3, r3, near, full,
     halo_send, halo_recv, sum_send, sum_recv,
 ):
     n_lon, n_lat, n_dp, rows, cols, ch = sizes
@@ -166,10 +166,10 @@
         right = jnp.concatenate([w_ref[t] for t in range(9)], 1)
         return product(left, right, NT)
 
-    def back_conv(e, z, w_ref, after=((), ())):
+    def back_conv(e, z, w_ref, halves=(0, 1), after=((), ())):
         step = (rows + 2) // 2
         size = step * cols
-        for i in range(2):
+        for i in halves:
             left = jnp.concatenate(
                 [z[i * size + (2 - r) * cols : i * size + (2 - r) * cols + size, :] for r in range(3)], 1
             )
@@ -199,7 +199,8 @@
                     cell_out[e, 4 + 2 * slot, 0:1, :] = first
                     cell_out[e, 5 + 2 * slot, 0:1, :] = last
             advance(*after[i])
-        halo_start(e)
+        if 1 in halves:
+            halo_start(e)
 
     def returned_row(e, h):
         value = q[h * cols : (h + 1) * cols, :]
@@ -226,6 +227,12 @@
 
     plane = ny * n_lat
 
+    def y_place(k):
+        return lax.rem(y + k, ny)
+
+    def lat_place(k):
+        return lax.rem(lat + k, n_lat)
+
     def plane_place(k):
         return lax.rem(y + k // n_lat, ny) * n_lat + lax.rem(lat + k % n_lat, n_lat)
 
@@ -238,6 +245,10 @@
             to = {"lon": lon, "lat": lat, "dp": dp}
             if axis == "core":
                 to["dp"] = y * 2 + 1 - core
+            elif axis == "y":
+                to["dp"] = lax.rem(y + k, ny) * 2 + core
+            elif axis == "lat":
+                to["lat"] = lax.rem(lat + k, n_lat)
             elif axis == "plane":
                 to["dp"] = lax.rem(y + k // n_lat, ny) * 2 + core
                 to["lat"] = lax.rem(lat + k % n_lat, n_lat)
@@ -259,18 +270,27 @@
         yield
         finish(copies)
         total = a0[p, rows_of(core * half, half), :] + r0[p]
-        a1[p] = total
-        s1[p] = total.astype(BF16)
-        copies = []
-        for k in range(1, plane):
-            there = rows_of(plane_place(k) * piece, piece)
-            copies.append(send(s1.at[p, there, :], r1.at[p, (k - 1) * piece : k * piece, :], "plane", k))
-        yield
-        finish(copies)
-        total = a1[p, rows_of(plane_place(0) * piece, piece), :]
-        for k in range(1, plane):
-            total = total + r1[p, (k - 1) * piece : k * piece, :].astype(F32)
-        at2 = core * half + plane_place(0) * piece
+        if p < 3:
+            rounds = (("y", ny, y_place), ("lat", n_lat, lat_place))[:: 1 if p % 2 == 0 else -1]
+        else:
+            rounds = (("plane", plane, plane_place),)
+        size, at2 = half, core * half
+        trail = []
+        for (axis, count, place), (kept, sent, got) in zip(rounds, ((a1, s1, r1), (a2, s2, r2))):
+            kept[p, 0:size, :] = total
+            sent[p, 0:size, :] = total.astype(BF16)
+            size //= count
+            copies = []
+            for k in range(1, count):
+                there = rows_of(place(k) * size, size)
+                copies.append(send(sent.at[p, there, :], got.at[p, (k - 1) * size : k * size, :], axis, k))
+            yield
+            finish(copies)
+            total = kept[p, rows_of(place(0) * size, size), :]
+            for k in range(1, count):
+                total = total + got[p, (k - 1) * size : k * size, :].astype(F32)
+            at2 = at2 + place(0) * size
+            trail.append((axis, count, at2, size))
         if scattered:
             a3[p] = total
             copies = []
@@ -296,15 +316,16 @@
             for k in range(1, n_lon):
                 total = total + near[p, k].astype(F32)
             target[rows_of(at2, piece), :] = total.astype(BF16)
-        own = target.at[rows_of(at2, piece), :]
-        copies = [send(own, own, "plane", k) for k in range(1, plane)]
-        yield
-        finish(copies)
+        for axis, count, at, size in reversed(trail):
+            own = target.at[rows_of(at, size), :]
+            copies = [send(own, own, axis, k) for k in range(1, count)]
+            yield
+            finish(copies)
         own = target.at[rows_of(core * half, half), :]
         copies = [send(own, own, "core")]
         yield
         finish(copies)
-        result = o1_ref if p < 3 else o2_ref
+        result = o2_ref if p < 3 else o1_ref
         for n in range(6):
             result[3 * (p % 3) + n // 2, :, (n % 2) * lanes : (n % 2 + 1) * lanes] = full[
                 p, n * ch : (n + 1) * ch, :
@@ -331,7 +352,7 @@
         gt[:, h * cols : (h + 1) * cols] = value.astype(F32).T.astype(BF16)
     pl.semaphore_wait(barrier, greeted)
     send_field(0, x_ref)
-    back_conv(2, gz, w2_ref)
+    back_conv(2, gz, w2_ref, (0,))
 
     pad_field(0, x_ref, x1)
     for i in range(2):
@@ -342,22 +363,25 @@
         slope[at, :] = sigma * (1.0 + value * (1.0 - sigma))
     send_field(1, act)
 
+    back_conv(2, gz, w2_ref, (1,))
+
+    pad_field(1, act, x2)
+    for r, ready in enumerate(((), (), (0,))):
+        begin(r, product(gt[...], x2[r * cols : r * cols + cells, :], NN))
+        advance(*ready)
     halo_wait(2)
     for h in range(rows):
         back = returned_row(2, h) * slope[h * cols : (h + 1) * cols, :]
         bz[(h + 2) * cols : (h + 3) * cols, :] = back.astype(BF16)
         bt[:, h * cols : (h + 1) * cols] = back.T.astype(BF16)
-
-    for r, ready in enumerate(((), (), (0,))):
-        begin(r, product(bt[...], x1[r * cols : r * cols + cells, :], NN))
+        if h == rows // 2:
+            advance(1)
+    advance(2)
+    for r, ready in enumerate(((), (0, 1), (3, 2))):
+        begin(3 + r, product(bt[...], x1[r * cols : r * cols + cells, :], NN))
         advance(*ready)
-    pad_field(1, act, x2)
-    advance(1)
-    for r, ready in enumerate(((2,), (0,), (3,))):
-        begin(3 + r, product(gt[...], x2[r * cols : r * cols + cells, :], NN))
-        advance(*ready)
-    back_conv(3, bz, w1_ref, ((4, 5, 1), (0, 2)))
-    for i, ready in enumerate(((1, 3), (0, 2, 4))):
+    back_conv(3, bz, w1_ref, after=((4, 5, 0), (3, 1, 2)))
+    for i, ready in enumerate(((4, 0), (5, 1))):
         at = slice(i * block, (i + 1) * block)
         out_ref[at, :] = (x_ref[at, :].astype(F32) + conv(x2, w2_ref, i)).astype(BF16)
         advance(*ready)
@@ -365,6 +389,7 @@
     for h in range(rows):
         at = slice(h * cols, (h + 1) * cols)
         gf_ref[at, :] = (g_ref[at, :].astype(F32) + returned_row(3, h)).astype(BF16)
+    advance(3, 2, 0)
     while running:
         advance(*sorted(running, reverse=True))
 
@@ -380,7 +405,7 @@
     part, half, lanes = 3 * ch, 3 * ch, ch // 2
     piece = half // (ny * n_lat)
     strip = max(8, piece // n_lon)
-    copies = 2 * (ny * n_lat + n_lon)
+    copies = 2 * (ny * n_lat + ny + n_lat + n_lon)
     vmem = pl.BlockSpec(memory_space=pltpu.VMEM)
     padded = ((rows + 2) * cols, part)
     zeroed = ((rows + 4) * cols, ch)
@@ -399,6 +424,8 @@
             pltpu.VMEM((4, 2, cols, ch), BF16), pltpu.VMEM((4, 2, cols, ch), BF16),
             pltpu.VMEM((6, 6 * ch, lanes), F32), pltpu.VMEM((6, half, lanes), F32),
             pltpu.VMEM((6, half, lanes), BF16), pltpu.VMEM((6, half, lanes), F32), pltpu.VMEM((6, half, lanes), BF16),
+            pltpu.VMEM((6, half // 2, lanes), BF16), pltpu.VMEM((6, half // 2, lanes), F32),
+            pltpu.VMEM((6, half // 2, lanes), BF16),
             pltpu.VMEM((6, piece, lanes), F32), pltpu.VMEM((6, n_lon - 1, strip, lanes), F32),
             pltpu.VMEM((6, n_lon, piece, lanes), BF16), pltpu.VMEM((6, 6 * ch, lanes), BF16),
             pltpu.SemaphoreType.DMA((4, 8)), pltpu.SemaphoreType.DMA((4, 8)),

time: 63.8 us -> 74 us (1.16)
  Pallas kernels: 55 us -> 65.2 us
    pallas_call x1, Pallas kernels: 55 us -> 65.2 us  [per_device(): pl.pallas_call(functools.partial(kernel, (n_lon, n_lat, n_dp, rows, cols,...]
where the time goes in v5:
time: 74 us; the launch traced here: 73.8 us
  Pallas kernels  65.2 us (88%)
  local copies, waits for them, and re-layouts  4.67 us (6%)
  other arithmetic  3.26 us (4%)
    pallas_call x1, Pallas kernels, per_device(): pl.pallas_call(functools.partial(kernel, (n_lon, n_lat, n_dp, rows, cols,...  65.2 us
    transpose x2, local copies, waits for them, and re-layouts, by_cells(): return jnp.transpose(array[0], (1, 2, 0)).reshape(cells, ch)  2.5 us
    reshape x2, local copies, waits for them, and re-layouts, by_channels(): return jnp.transpose(array.reshape(rows, cols, ch), (2, 0, 1))[None]  2.15 us
    convert_element_type x1, other arithmetic, per_device(): grad_one.astype(F32)  1.63 us
    convert_element_type x1, other arithmetic, per_device(): grad_two.astype(F32)  1.63 us

profile of v5, /device:TPU:0, one launch (start us, length us, event | category | flops | bytes accessed | tf_op | source)
XLA Modules:
  0.0 73.8 jit_solution(4901370816812973707)
XLA Ops:
  0.6 0.0 copy-start.3
  0.6 0.0 copy-start
  0.7 1.4 %copy.9 = bf16[8,128,256]{2,1,0:T(8,128)(2,1)S(1)} copy(bf16[8,128,256]{1,0,2:T(8,128)(2,1)} %bitcast.19) | data formatting | bytes 1048576 | tf_op jit(solution)/shard_map/transpose | solution.py:403
  2.0 0.0 copy-done.3
  2.0 1.1 %copy.10 = bf16[8,128,256]{2,1,0:T(8,128)(2,1)} copy(bf16[8,128,256]{1,0,2:T(8,128)(2,1)S(1)} %bitcast.20) | data formatting | bytes 1048576 | tf_op jit(solution)/shard_map/transpose | solution.py:403
  3.2 0.0 copy-done
  3.2 65.2 %shard_map.84 = (bf16[1024,256]{1,0:T(8,128)(2,1)S(1)}, bf16[1024,256]{1,0:T(8,128)(2,1)S(1)}, bf16[9,256,256]{2,1,0:T(8,128)(2,1)}, bf16[9,256,256]{2,1,0:T(8,128)(2,1)}) custom-call(bf16[1024,256]{1,0:T(8,128)(2,1)S(1)} %bitcast.18, bf16[1024,256]{1,0:T(8,128)(2,1)} %bitcast.23, bf16[9,256,256]{2,1,0:T(8,128)(2,1)} %w1_ref.1, bf16[9,256,256]{2,1,0:T(8,128)(2,1)} %w2_ref.1, ...), custom_call_target="tpu_custom_call" | custom-call | flops 7247757312 | bytes 4718592 | tf_op jit(solution)/shard_map/pallas_call | solution.py:412
  68.4 0.0 copy-start.2
  68.4 1.1 %copy.11 = bf16[8,128,256]{1,0,2:T(8,128)(2,1)} copy(bf16[8,128,256]{2,1,0:T(8,128)(2,1)S(1)} %bitcast.17) | data formatting | bytes 1048576 | tf_op jit(solution)/shard_map/reshape | solution.py:443
  69.5 1.1 %copy.12 = bf16[8,128,256]{1,0,2:T(8,128)(2,1)} copy(bf16[8,128,256]{2,1,0:T(8,128)(2,1)S(1)} %bitcast.16) | data formatting | bytes 1048576 | tf_op jit(solution)/shard_map/reshape | solution.py:443
  70.6 0.0 copy-done.2
  70.6 0.0 copy-start.1
  70.6 1.6 %convert_element_type.6 = f32[9,256,256]{2,1,0:T(8,128)} convert(bf16[9,256,256]{2,1,0:T(8,128)(2,1)S(1)} %copy-done.2) | non-fusion elementwise | flops 589824 | bytes 3538944 | tf_op jit(solution)/shard_map/convert_element_type | solution.py:448
  72.2 0.0 copy-done.1
  72.2 1.6 %convert_element_type.7 = f32[9,256,256]{2,1,0:T(8,128)} convert(bf16[9,256,256]{2,1,0:T(8,128)(2,1)S(1)} %copy-done.1) | non-fusion elementwise | flops 589824 | bytes 3538944 | tf_op jit(solution)/shard_map/convert_element_type | solution.py:449
Async XLA Ops:
  0.6 1.4 %copy-start.3 = (bf16[1,256,8,128]{3,2,1,0:T(8,128)(2,1)S(1)}, bf16[1,256,8,128]{3,2,1,0:T(8,128)(2,1)}, u32[]{:S(2)}) copy-start(bf16[1,256,8,128]{3,2,1,0:T(8,128)(2,1)} %param.9) | copy-start | bytes 1572868
  0.6 2.5 %copy-start = (s32[1,4]{1,0:T(1,128)S(1)}, s32[1,4]{1,0:T(1,128)}, u32[]{:S(2)}) copy-start(s32[1,4]{1,0:T(1,128)} %flip_ref.1) | copy-start | bytes 52
  68.4 2.2 %copy-start.2 = (bf16[9,256,256]{2,1,0:T(8,128)(2,1)S(1)}, bf16[9,256,256]{2,1,0:T(8,128)(2,1)}, u32[]{:S(2)}) copy-start(bf16[9,256,256]{2,1,0:T(8,128)(2,1)} %get-tuple-element.10) | copy-start | bytes 3538948
  70.6 1.6 %copy-start.1 = (bf16[9,256,256]{2,1,0:T(8,128)(2,1)S(1)}, bf16[9,256,256]{2,1,0:T(8,128)(2,1)}, u32[]{:S(2)}) copy-start(bf16[9,256,256]{2,1,0:T(8,128)(2,1)} %get-tuple-element.11) | copy-start | bytes 3538948

commit v6 on v4

--- a/solution.py
+++ b/solution.py
@@ -271,7 +271,7 @@
         for k in range(1, plane):
             total = total + r1[p, (k - 1) * piece : k * piece, :].astype(F32)
         at2 = core * half + plane_place(0) * piece
-        if scattered:
+        if scattered and p < 4:
             a3[p] = total
             copies = []
             for k in range(1, n_lon):
@@ -353,11 +353,11 @@
         advance(*ready)
     pad_field(1, act, x2)
     advance(1)
-    for r, ready in enumerate(((2,), (0,), (3,))):
+    for r, ready in enumerate(((2,), (), (3,))):
         begin(3 + r, product(gt[...], x2[r * cols : r * cols + cells, :], NN))
         advance(*ready)
-    back_conv(3, bz, w1_ref, ((4, 5, 1), (0, 2)))
-    for i, ready in enumerate(((1, 3), (0, 2, 4))):
+    back_conv(3, bz, w1_ref, ((5, 4, 0, 1), (2,)))
+    for i, ready in enumerate(((3, 0), (4, 1))):
         at = slice(i * block, (i + 1) * block)
         out_ref[at, :] = (x_ref[at, :].astype(F32) + conv(x2, w2_ref, i)).astype(BF16)
         advance(*ready)

time: 63.8 us -> 67.6 us (1.060)
  Pallas kernels: 55 us -> 58.9 us
    pallas_call x1, Pallas kernels: 55 us -> 58.9 us  [per_device(): pl.pallas_call(functools.partial(kernel, (n_lon, n_lat, n_dp, rows, cols,...]
where the time goes in v6:
time: 67.6 us; the launch traced here: 67.5 us
  Pallas kernels  58.9 us (87%)
  local copies, waits for them, and re-layouts  4.67 us (7%)
  other arithmetic  3.26 us (5%)
  between operations  0.68 us (1%)
    pallas_call x1, Pallas kernels, per_device(): pl.pallas_call(functools.partial(kernel, (n_lon, n_lat, n_dp, rows, cols,...  58.9 us
    transpose x2, local copies, waits for them, and re-layouts, by_cells(): return jnp.transpose(array[0], (1, 2, 0)).reshape(cells, ch)  2.5 us
    reshape x2, local copies, waits for them, and re-layouts, by_channels(): return jnp.transpose(array.reshape(rows, cols, ch), (2, 0, 1))[None]  2.15 us
    convert_element_type x1, other arithmetic, per_device(): grad_one.astype(F32)  1.63 us
    convert_element_type x1, other arithmetic, per_device(): grad_two.astype(F32)  1.63 us

profile of v6, /device:TPU:0, one launch (start us, length us, event | category | flops | bytes accessed | tf_op | source)
XLA Modules:
  0.0 67.5 jit_solution(12467720634376082272)
XLA Ops:
  0.6 0.0 copy-start.3
  0.6 0.0 copy-start
  0.7 1.4 %copy.9 = bf16[8,128,256]{2,1,0:T(8,128)(2,1)S(1)} copy(bf16[8,128,256]{1,0,2:T(8,128)(2,1)} %bitcast.19) | data formatting | bytes 1048576 | tf_op jit(solution)/shard_map/transpose | solution.py:378
  2.0 0.0 copy-done.3
  2.0 1.1 %copy.10 = bf16[8,128,256]{2,1,0:T(8,128)(2,1)} copy(bf16[8,128,256]{1,0,2:T(8,128)(2,1)S(1)} %bitcast.20) | data formatting | bytes 1048576 | tf_op jit(solution)/shard_map/transpose | solution.py:378
  3.2 0.0 copy-done
  3.2 58.9 %shard_map.84 = (bf16[1024,256]{1,0:T(8,128)(2,1)S(1)}, bf16[1024,256]{1,0:T(8,128)(2,1)S(1)}, bf16[9,256,256]{2,1,0:T(8,128)(2,1)}, bf16[9,256,256]{2,1,0:T(8,128)(2,1)}) custom-call(bf16[1024,256]{1,0:T(8,128)(2,1)S(1)} %bitcast.18, bf16[1024,256]{1,0:T(8,128)(2,1)} %bitcast.23, bf16[9,256,256]{2,1,0:T(8,128)(2,1)} %w1_ref.1, bf16[9,256,256]{2,1,0:T(8,128)(2,1)} %w2_ref.1, ...), custom_call_target="tpu_custom_call" | custom-call | flops 7247757312 | bytes 4718592 | tf_op jit(solution)/shard_map/pallas_call | solution.py:387
  62.0 0.0 copy-start.2
  62.0 1.1 %copy.11 = bf16[8,128,256]{1,0,2:T(8,128)(2,1)} copy(bf16[8,128,256]{2,1,0:T(8,128)(2,1)S(1)} %bitcast.17) | data formatting | bytes 1048576 | tf_op jit(solution)/shard_map/reshape | solution.py:416
  63.1 1.1 %copy.12 = bf16[8,128,256]{1,0,2:T(8,128)(2,1)} copy(bf16[8,128,256]{2,1,0:T(8,128)(2,1)S(1)} %bitcast.16) | data formatting | bytes 1048576 | tf_op jit(solution)/shard_map/reshape | solution.py:416
  64.2 0.0 copy-done.2
  64.2 0.0 copy-start.1
  64.2 1.6 %convert_element_type.6 = f32[9,256,256]{2,1,0:T(8,128)} convert(bf16[9,256,256]{2,1,0:T(8,128)(2,1)S(1)} %copy-done.2) | non-fusion elementwise | flops 589824 | bytes 3538944 | tf_op jit(solution)/shard_map/convert_element_type | solution.py:421
  65.8 0.0 copy-done.1
  65.8 1.6 %convert_element_type.7 = f32[9,256,256]{2,1,0:T(8,128)} convert(bf16[9,256,256]{2,1,0:T(8,128)(2,1)S(1)} %copy-done.1) | non-fusion elementwise | flops 589824 | bytes 3538944 | tf_op jit(solution)/shard_map/convert_element_type | solution.py:422
Async XLA Ops:
  0.6 1.4 %copy-start.3 = (bf16[1,256,8,128]{3,2,1,0:T(8,128)(2,1)S(1)}, bf16[1,256,8,128]{3,2,1,0:T(8,128)(2,1)}, u32[]{:S(2)}) copy-start(bf16[1,256,8,128]{3,2,1,0:T(8,128)(2,1)} %param.9) | copy-start | bytes 1572868
  0.6 2.5 %copy-start = (s32[1,4]{1,0:T(1,128)S(1)}, s32[1,4]{1,0:T(1,128)}, u32[]{:S(2)}) copy-start(s32[1,4]{1,0:T(1,128)} %flip_ref.1) | copy-start | bytes 52
  62.0 2.2 %copy-start.2 = (bf16[9,256,256]{2,1,0:T(8,128)(2,1)S(1)}, bf16[9,256,256]{2,1,0:T(8,128)(2,1)}, u32[]{:S(2)}) copy-start(bf16[9,256,256]{2,1,0:T(8,128)(2,1)} %get-tuple-element.10) | copy-start | bytes 3538948
  64.2 1.6 %copy-start.1 = (bf16[9,256,256]{2,1,0:T(8,128)(2,1)S(1)}, bf16[9,256,256]{2,1,0:T(8,128)(2,1)}, u32[]{:S(2)}) copy-start(bf16[9,256,256]{2,1,0:T(8,128)(2,1)} %get-tuple-element.11) | copy-start | bytes 3538948
